TPU v7x, 128 devices: a whole 4x4x4 slice. The times are simulated.
128 devices in a mesh: section: 8 (over z, core), group: 16 (over x, y).
Axes of the slice: x: 4, y: 4, z: 4, core: 2. Of those that a mesh axis runs over, the one named last changes fastest.
Arguments:
- features: bfloat16 [65536, 256], P('group'), may hold values from -6 to 6
- history: bfloat16 [8, 65536, 256], P('section', 'group'), may hold values from -6 to 6
- halo_blocks: int32 [16, 16, 1], P('group'), may hold values from 0 to 31
- tile_values: bfloat16 [128, 32, 128, 128], P('group'), may hold values from -0.1875 to 0.1875
- tile_dst: int32 [128, 32], P('group'), may hold values from 0 to 3
- tile_src: int32 [128, 32], P('group'), may hold values from 0 to 19
- w_self: bfloat16 [8, 256, 256], P('section'), may hold values from -0.375 to 0.375
- w_neigh: bfloat16 [8, 256, 256], P('section'), may hold values from -0.375 to 0.375
- bias: float32 [8, 256], P('section'), may hold values from -3 to 3
- gain: float32 [8, 256], P('section'), may hold values from 0.25 to 1.75
Outputs:
- embeddings: bfloat16 [65536, 256], P('group', 'section')
- fresh_history: bfloat16 [8, 65536, 256], P('section', 'group')
All inputs are finite; a program needn't handle non-finite values.
Results may differ from a plain program's by a relative error of at most 0.014.
Values may be sent and summed in bfloat16 or wider, within the bound.
A program may use at most 128 MiB of HBM per device.

v0:
```python
import jax
import jax.numpy as jnp
from jax import lax
from jax.sharding import PartitionSpec as P


def shifted(block, axis, distance):
    devices = range(lax.axis_size(axis))
    route = [(i - distance, i) for i in devices if i - distance in devices]
    return lax.ppermute(block, axis, route)


def spread(array, axis, root):
    mine = lax.axis_index(axis) == root
    return lax.psum(jnp.where(mine, array, jnp.zeros_like(array)), axis)


def sage_layer(
    inputs, halo, tiles, targets, source_ids, weight_self, weight_neigh, bias_row, gain_row
):
    width = inputs.shape[1]
    tile_rows = tiles.shape[1]
    block_count = inputs.shape[0] // tile_rows
    stacked = jnp.concatenate([inputs, halo], axis=0)
    blocks = stacked.reshape(-1, tile_rows, width)
    picked = jnp.take(blocks, source_ids, axis=0)
    products = jnp.einsum("tij,tjh->tih", tiles, picked, preferred_element_type=jnp.float32)
    onehot = (targets[None, :] == jnp.arange(block_count, dtype=jnp.int32)[:, None]).astype(
        jnp.float32
    )
    aggregate = (
        jnp.einsum("bt,tih->bih", onehot, products)
        .reshape(inputs.shape[0], width)
        .astype(jnp.bfloat16)
    )
    pre = jnp.dot(inputs, weight_self, preferred_element_type=jnp.float32)
    pre = pre + jnp.dot(aggregate, weight_neigh, preferred_element_type=jnp.float32) + bias_row
    center = pre - jnp.mean(pre, axis=1, keepdims=True)
    variance = jnp.mean(center * center, axis=1, keepdims=True)
    normed = center * lax.rsqrt(variance + 1e-05) * gain_row
    return (inputs.astype(jnp.float32) + jax.nn.relu(normed)).astype(jnp.bfloat16)


def per_device(
    features, history, halo_blocks, tile_values, tile_dst, tile_src, w_self, w_neigh, bias, gain
):
    groups = lax.axis_size("group")
    sections = lax.axis_size("section")
    section_id = lax.axis_index("section")
    width = features.shape[1]
    tile_rows = tile_values.shape[2]
    micro_count = tile_values.shape[0]
    micro_rows = features.shape[0] // micro_count
    local_hist = history[0]
    wanted = halo_blocks[0]
    offsets = jnp.arange(tile_rows, dtype=jnp.int32)
    everything = lax.all_gather(local_hist, "group", axis=0, tiled=True)
    starts = jnp.arange(groups, dtype=jnp.int32)[:, None] * local_hist.shape[0] + wanted * tile_rows
    row_ids = (starts[:, :, None] + offsets).reshape(-1)
    halo = jnp.take(everything, row_ids, axis=0)
    blocks_in = features.reshape(micro_count, micro_rows, width)
    weight_self = w_self[0]
    weight_neigh = w_neigh[0]
    bias_row = bias[0]
    gain_row = gain[0]

    def advance(step, carry):
        incoming, fresh, finals = carry
        micro = step - section_id
        valid = jnp.logical_and(micro >= 0, micro < micro_count)
        position = jnp.clip(micro, 0, micro_count - 1)
        own_rows = lax.dynamic_index_in_dim(blocks_in, position, 0, keepdims=False)
        inputs = jnp.where(section_id == 0, own_rows, incoming)
        tiles = lax.dynamic_index_in_dim(tile_values, position, 0, keepdims=False)
        targets = lax.dynamic_index_in_dim(tile_dst, position, 0, keepdims=False)
        source_ids = lax.dynamic_index_in_dim(tile_src, position, 0, keepdims=False)
        output = sage_layer(
            inputs, halo, tiles, targets, source_ids, weight_self, weight_neigh, bias_row, gain_row
        )
        fresh = jnp.where(valid, lax.dynamic_update_index_in_dim(fresh, inputs, position, 0), fresh)
        finals = jnp.where(
            valid, lax.dynamic_update_index_in_dim(finals, output, position, 0), finals
        )
        passed = shifted(output, "section", 1)
        return (passed, fresh, finals)

    empty_rows = jnp.zeros((micro_rows, width), jnp.bfloat16)
    empty_all = jnp.zeros((micro_count, micro_rows, width), jnp.bfloat16)
    passed, fresh, finals = lax.fori_loop(
        0, micro_count + sections - 1, advance, (empty_rows, empty_all, empty_all)
    )
    share = width // sections
    last_rows = spread(finals.reshape(-1, width), "section", sections - 1)
    embeddings = lax.dynamic_slice_in_dim(last_rows, section_id * share, share, 1)
    return (embeddings, fresh.reshape(1, -1, width))


def solution(mesh):
    placed = (
        P("group", None),
        P("section", "group", None),
        P("group", None, None),
        P("group", None, None, None),
        P("group", None),
        P("group", None),
        P("section", None, None),
        P("section", None, None),
        P("section", None),
        P("section", None),
    )
    return jax.shard_map(
        per_device,
        mesh=mesh,
        in_specs=placed,
        out_specs=(P("group", "section"), P("section", "group", None)),
        check_vma=False,
    )
```

profile of v0, /device:TPU:1, one launch (start us, length us, event | category | flops | bytes accessed | tf_op | source)
XLA Modules:
  0.0 600.5 jit_solution(2650306110506115265)
XLA Ops:
  8.2 202.1 %all-gather.3.cloned.1.call-done = bf16[1,65536,256]{2,1,0:T(8,128)(2,1)} async-done(((bf16[1,4096,256]{2,1,0:T(8,128)(2,1)}), bf16[1,65536,256]{2,1,0:T(8,128)(2,1)}) %all-gather.3.cloned.1.call-update) | async-done | bytes 33554448 | tf_op jit(solution)/shard_map/all_gather | solution.py:57
  210.3 21.9 %gather_fusion.1 = bf16[2048,256]{1,0:T(8,128)(2,1)S(1)} fusion(bf16[65536,256]{1,0:T(8,128)(2,1)} %bitcast.83, s32[2048]{0:T(1024)S(1)} %broadcast_clamp_fusion), kind=kCustom, calls=%fused_computation.1 | custom fusion | bytes 2105344 | tf_op jit(solution)/shard_map/jit(_take)/gather | solution.py:60
  235.8 289.8 %while.18 = (s32[]{:T(128)}, bf16[512,256]{0,1:T(8,128)(2,1)S(1)}, bf16[8,512,256]{2,1,0:T(8,128)(2,1)}, bf16[8,512,256]{1,2,0:T(8,128)(2,1)}, pred[]{:T(512)}, ...) while((s32[]{:T(128)}, bf16[512,256]{0,1:T(8,128)(2,1)S(1)}, ...), condition=%wide.region_3.4_spmd, body=%wide.region_0.3_spmd.sunk | while | flops 416810912 | bytes 37513264 | solution.py:89
  247.5 3.7 collective-permute-start
  252.1 2.4 collective-permute-done
  266.2 4.4 collective-permute-start
  271.5 2.4 collective-permute-done
  285.6 4.4 collective-permute-start
  290.8 2.4 collective-permute-done
  304.9 4.4 collective-permute-start
  310.2 2.4 collective-permute-done
  324.3 4.4 collective-permute-start
  329.5 2.4 collective-permute-done
  343.6 4.4 collective-permute-start
  348.9 2.4 collective-permute-done
  363.0 4.4 collective-permute-start
  368.3 2.4 collective-permute-done
  382.4 4.4 collective-permute-start
  387.6 2.4 collective-permute-done
  401.7 4.4 collective-permute-start
  407.0 2.4 collective-permute-done
  421.1 4.4 collective-permute-start
  426.3 2.4 collective-permute-done
  440.4 4.4 collective-permute-start
  445.7 2.4 collective-permute-done
  459.8 4.4 collective-permute-start
  465.1 2.4 collective-permute-done
  479.2 4.4 collective-permute-start
  498.6 4.4 collective-permute-start
  517.9 4.4 collective-permute-start
  523.2 2.4 collective-permute-done
  527.4 64.6 %all-reduce.2.cloned.1.call-done = bf16[4096,256]{0,1:T(8,128)(2,1)} async-done(((bf16[4096,256]{0,1:T(8,128)(2,1)}), bf16[4096,256]{0,1:T(8,128)(2,1)}) %all-reduce.2.cloned.1.call-update) | async-done | bytes 2097168 | tf_op jit(solution)/shard_map/psum | solution.py:15
  (566 shorter events, 198.5 us)
Async XLA Ops:
  7.2 203.2 %all-gather.3.cloned.1.call-start = ((), (), s32[]{:S(2)}) async-start(), calls=%async_computation.1 | async-start | bytes 35651584 | tf_op jit(solution)/shard_map/all_gather | solution.py:57
  7.9 584.1 %all-reduce.2.cloned.1.call-start = ((), (), s32[]{:S(2)}) async-start(), calls=%async_computation | async-start | bytes 4194304 | tf_op jit(solution)/shard_map/psum | solution.py:15
  245.2 9.3 %copy-start.3 = (bf16[2048,256]{1,0:T(8,128)(2,1)S(1)}, bf16[2048,256]{1,0:T(8,128)(2,1)}, u32[]{:S(2)}) copy-start(bf16[2048,256]{1,0:T(8,128)(2,1)} %copy-done.2) | copy-start | bytes 3145732 | tf_op jit(solution)/shard_map/while
  247.5 7.0 %collective-permute-start = (bf16[512,256]{0,1:T(8,128)(2,1)S(1)}, bf16[512,256]{0,1:T(8,128)(2,1)S(1)}, u32[]{:S(2)}, u32[]{:S(2)}) collective-permute-start(bf16[512,256]{0,1:T(8,128)(2,1)S(1)} %get-tuple-element.452), channel_id=1, source_target_pairs={{0,16},{16,32},{32,48},{48,64},{64,80},{80,96},{96,112},{1,17},{17... | collective-permute-start | bytes 786440 | tf_op jit(solution)/shard_map/while/body/eval_jaxpr/ppermute | solution.py:10
  263.9 9.9 %copy-start.3 = (bf16[2048,256]{1,0:T(8,128)(2,1)S(1)}, bf16[2048,256]{1,0:T(8,128)(2,1)}, u32[]{:S(2)}) copy-start(bf16[2048,256]{1,0:T(8,128)(2,1)} %copy-done.2) | copy-start | bytes 3145732 | tf_op jit(solution)/shard_map/while
  266.2 7.7 %collective-permute-start = (bf16[512,256]{0,1:T(8,128)(2,1)S(1)}, bf16[512,256]{0,1:T(8,128)(2,1)S(1)}, u32[]{:S(2)}, u32[]{:S(2)}) collective-permute-start(bf16[512,256]{0,1:T(8,128)(2,1)S(1)} %get-tuple-element.452), channel_id=1, source_target_pairs={{0,16},{16,32},{32,48},{48,64},{64,80},{80,96},{96,112},{1,17},{17... | collective-permute-start | bytes 786440 | tf_op jit(solution)/shard_map/while/body/eval_jaxpr/ppermute | solution.py:10
  283.3 9.9 %copy-start.3 = (bf16[2048,256]{1,0:T(8,128)(2,1)S(1)}, bf16[2048,256]{1,0:T(8,128)(2,1)}, u32[]{:S(2)}) copy-start(bf16[2048,256]{1,0:T(8,128)(2,1)} %copy-done.2) | copy-start | bytes 3145732 | tf_op jit(solution)/shard_map/while
  285.6 7.7 %collective-permute-start = (bf16[512,256]{0,1:T(8,128)(2,1)S(1)}, bf16[512,256]{0,1:T(8,128)(2,1)S(1)}, u32[]{:S(2)}, u32[]{:S(2)}) collective-permute-start(bf16[512,256]{0,1:T(8,128)(2,1)S(1)} %get-tuple-element.452), channel_id=1, source_target_pairs={{0,16},{16,32},{32,48},{48,64},{64,80},{80,96},{96,112},{1,17},{17... | collective-permute-start | bytes 786440 | tf_op jit(solution)/shard_map/while/body/eval_jaxpr/ppermute | solution.py:10
  302.6 10.0 %copy-start.3 = (bf16[2048,256]{1,0:T(8,128)(2,1)S(1)}, bf16[2048,256]{1,0:T(8,128)(2,1)}, u32[]{:S(2)}) copy-start(bf16[2048,256]{1,0:T(8,128)(2,1)} %copy-done.2) | copy-start | bytes 3145732 | tf_op jit(solution)/shard_map/while
  304.9 7.7 %collective-permute-start = (bf16[512,256]{0,1:T(8,128)(2,1)S(1)}, bf16[512,256]{0,1:T(8,128)(2,1)S(1)}, u32[]{:S(2)}, u32[]{:S(2)}) collective-permute-start(bf16[512,256]{0,1:T(8,128)(2,1)S(1)} %get-tuple-element.452), channel_id=1, source_target_pairs={{0,16},{16,32},{32,48},{48,64},{64,80},{80,96},{96,112},{1,17},{17... | collective-permute-start | bytes 786440 | tf_op jit(solution)/shard_map/while/body/eval_jaxpr/ppermute | solution.py:10
  322.0 10.0 %copy-start.3 = (bf16[2048,256]{1,0:T(8,128)(2,1)S(1)}, bf16[2048,256]{1,0:T(8,128)(2,1)}, u32[]{:S(2)}) copy-start(bf16[2048,256]{1,0:T(8,128)(2,1)} %copy-done.2) | copy-start | bytes 3145732 | tf_op jit(solution)/shard_map/while
  324.3 7.7 %collective-permute-start = (bf16[512,256]{0,1:T(8,128)(2,1)S(1)}, bf16[512,256]{0,1:T(8,128)(2,1)S(1)}, u32[]{:S(2)}, u32[]{:S(2)}) collective-permute-start(bf16[512,256]{0,1:T(8,128)(2,1)S(1)} %get-tuple-element.452), channel_id=1, source_target_pairs={{0,16},{16,32},{32,48},{48,64},{64,80},{80,96},{96,112},{1,17},{17... | collective-permute-start | bytes 786440 | tf_op jit(solution)/shard_map/while/body/eval_jaxpr/ppermute | solution.py:10
  341.3 10.0 %copy-start.3 = (bf16[2048,256]{1,0:T(8,128)(2,1)S(1)}, bf16[2048,256]{1,0:T(8,128)(2,1)}, u32[]{:S(2)}) copy-start(bf16[2048,256]{1,0:T(8,128)(2,1)} %copy-done.2) | copy-start | bytes 3145732 | tf_op jit(solution)/shard_map/while
  343.6 7.7 %collective-permute-start = (bf16[512,256]{0,1:T(8,128)(2,1)S(1)}, bf16[512,256]{0,1:T(8,128)(2,1)S(1)}, u32[]{:S(2)}, u32[]{:S(2)}) collective-permute-start(bf16[512,256]{0,1:T(8,128)(2,1)S(1)} %get-tuple-element.452), channel_id=1, source_target_pairs={{0,16},{16,32},{32,48},{48,64},{64,80},{80,96},{96,112},{1,17},{17... | collective-permute-start | bytes 786440 | tf_op jit(solution)/shard_map/while/body/eval_jaxpr/ppermute | solution.py:10
  360.7 10.0 %copy-start.3 = (bf16[2048,256]{1,0:T(8,128)(2,1)S(1)}, bf16[2048,256]{1,0:T(8,128)(2,1)}, u32[]{:S(2)}) copy-start(bf16[2048,256]{1,0:T(8,128)(2,1)} %copy-done.2) | copy-start | bytes 3145732 | tf_op jit(solution)/shard_map/while
  363.0 7.7 %collective-permute-start = (bf16[512,256]{0,1:T(8,128)(2,1)S(1)}, bf16[512,256]{0,1:T(8,128)(2,1)S(1)}, u32[]{:S(2)}, u32[]{:S(2)}) collective-permute-start(bf16[512,256]{0,1:T(8,128)(2,1)S(1)} %get-tuple-element.452), channel_id=1, source_target_pairs={{0,16},{16,32},{32,48},{48,64},{64,80},{80,96},{96,112},{1,17},{17... | collective-permute-start | bytes 786440 | tf_op jit(solution)/shard_map/while/body/eval_jaxpr/ppermute | solution.py:10
  380.1 10.0 %copy-start.3 = (bf16[2048,256]{1,0:T(8,128)(2,1)S(1)}, bf16[2048,256]{1,0:T(8,128)(2,1)}, u32[]{:S(2)}) copy-start(bf16[2048,256]{1,0:T(8,128)(2,1)} %copy-done.2) | copy-start | bytes 3145732 | tf_op jit(solution)/shard_map/while
  382.4 7.7 %collective-permute-start = (bf16[512,256]{0,1:T(8,128)(2,1)S(1)}, bf16[512,256]{0,1:T(8,128)(2,1)S(1)}, u32[]{:S(2)}, u32[]{:S(2)}) collective-permute-start(bf16[512,256]{0,1:T(8,128)(2,1)S(1)} %get-tuple-element.452), channel_id=1, source_target_pairs={{0,16},{16,32},{32,48},{48,64},{64,80},{80,96},{96,112},{1,17},{17... | collective-permute-start | bytes 786440 | tf_op jit(solution)/shard_map/while/body/eval_jaxpr/ppermute | solution.py:10
  399.4 10.0 %copy-start.3 = (bf16[2048,256]{1,0:T(8,128)(2,1)S(1)}, bf16[2048,256]{1,0:T(8,128)(2,1)}, u32[]{:S(2)}) copy-start(bf16[2048,256]{1,0:T(8,128)(2,1)} %copy-done.2) | copy-start | bytes 3145732 | tf_op jit(solution)/shard_map/while
  401.7 7.7 %collective-permute-start = (bf16[512,256]{0,1:T(8,128)(2,1)S(1)}, bf16[512,256]{0,1:T(8,128)(2,1)S(1)}, u32[]{:S(2)}, u32[]{:S(2)}) collective-permute-start(bf16[512,256]{0,1:T(8,128)(2,1)S(1)} %get-tuple-element.452), channel_id=1, source_target_pairs={{0,16},{16,32},{32,48},{48,64},{64,80},{80,96},{96,112},{1,17},{17... | collective-permute-start | bytes 786440 | tf_op jit(solution)/shard_map/while/body/eval_jaxpr/ppermute | solution.py:10
  418.8 10.0 %copy-start.3 = (bf16[2048,256]{1,0:T(8,128)(2,1)S(1)}, bf16[2048,256]{1,0:T(8,128)(2,1)}, u32[]{:S(2)}) copy-start(bf16[2048,256]{1,0:T(8,128)(2,1)} %copy-done.2) | copy-start | bytes 3145732 | tf_op jit(solution)/shard_map/while
  421.1 7.7 %collective-permute-start = (bf16[512,256]{0,1:T(8,128)(2,1)S(1)}, bf16[512,256]{0,1:T(8,128)(2,1)S(1)}, u32[]{:S(2)}, u32[]{:S(2)}) collective-permute-start(bf16[512,256]{0,1:T(8,128)(2,1)S(1)} %get-tuple-element.452), channel_id=1, source_target_pairs={{0,16},{16,32},{32,48},{48,64},{64,80},{80,96},{96,112},{1,17},{17... | collective-permute-start | bytes 786440 | tf_op jit(solution)/shard_map/while/body/eval_jaxpr/ppermute | solution.py:10
  438.2 10.0 %copy-start.3 = (bf16[2048,256]{1,0:T(8,128)(2,1)S(1)}, bf16[2048,256]{1,0:T(8,128)(2,1)}, u32[]{:S(2)}) copy-start(bf16[2048,256]{1,0:T(8,128)(2,1)} %copy-done.2) | copy-start | bytes 3145732 | tf_op jit(solution)/shard_map/while
  440.4 7.7 %collective-permute-start = (bf16[512,256]{0,1:T(8,128)(2,1)S(1)}, bf16[512,256]{0,1:T(8,128)(2,1)S(1)}, u32[]{:S(2)}, u32[]{:S(2)}) collective-permute-start(bf16[512,256]{0,1:T(8,128)(2,1)S(1)} %get-tuple-element.452), channel_id=1, source_target_pairs={{0,16},{16,32},{32,48},{48,64},{64,80},{80,96},{96,112},{1,17},{17... | collective-permute-start | bytes 786440 | tf_op jit(solution)/shard_map/while/body/eval_jaxpr/ppermute | solution.py:10
  457.5 10.0 %copy-start.3 = (bf16[2048,256]{1,0:T(8,128)(2,1)S(1)}, bf16[2048,256]{1,0:T(8,128)(2,1)}, u32[]{:S(2)}) copy-start(bf16[2048,256]{1,0:T(8,128)(2,1)} %copy-done.2) | copy-start | bytes 3145732 | tf_op jit(solution)/shard_map/while
  459.8 7.7 %collective-permute-start = (bf16[512,256]{0,1:T(8,128)(2,1)S(1)}, bf16[512,256]{0,1:T(8,128)(2,1)S(1)}, u32[]{:S(2)}, u32[]{:S(2)}) collective-permute-start(bf16[512,256]{0,1:T(8,128)(2,1)S(1)} %get-tuple-element.452), channel_id=1, source_target_pairs={{0,16},{16,32},{32,48},{48,64},{64,80},{80,96},{96,112},{1,17},{17... | collective-permute-start | bytes 786440 | tf_op jit(solution)/shard_map/while/body/eval_jaxpr/ppermute | solution.py:10
  476.9 10.0 %copy-start.3 = (bf16[2048,256]{1,0:T(8,128)(2,1)S(1)}, bf16[2048,256]{1,0:T(8,128)(2,1)}, u32[]{:S(2)}) copy-start(bf16[2048,256]{1,0:T(8,128)(2,1)} %copy-done.2) | copy-start | bytes 3145732 | tf_op jit(solution)/shard_map/while
  479.2 7.7 %collective-permute-start = (bf16[512,256]{0,1:T(8,128)(2,1)S(1)}, bf16[512,256]{0,1:T(8,128)(2,1)S(1)}, u32[]{:S(2)}, u32[]{:S(2)}) collective-permute-start(bf16[512,256]{0,1:T(8,128)(2,1)S(1)} %get-tuple-element.452), channel_id=1, source_target_pairs={{0,16},{16,32},{32,48},{48,64},{64,80},{80,96},{96,112},{1,17},{17... | collective-permute-start | bytes 786440 | tf_op jit(solution)/shard_map/while/body/eval_jaxpr/ppermute | solution.py:10
  496.3 10.0 %copy-start.3 = (bf16[2048,256]{1,0:T(8,128)(2,1)S(1)}, bf16[2048,256]{1,0:T(8,128)(2,1)}, u32[]{:S(2)}) copy-start(bf16[2048,256]{1,0:T(8,128)(2,1)} %copy-done.2) | copy-start | bytes 3145732 | tf_op jit(solution)/shard_map/while
  498.6 7.7 %collective-permute-start = (bf16[512,256]{0,1:T(8,128)(2,1)S(1)}, bf16[512,256]{0,1:T(8,128)(2,1)S(1)}, u32[]{:S(2)}, u32[]{:S(2)}) collective-permute-start(bf16[512,256]{0,1:T(8,128)(2,1)S(1)} %get-tuple-element.452), channel_id=1, source_target_pairs={{0,16},{16,32},{32,48},{48,64},{64,80},{80,96},{96,112},{1,17},{17... | collective-permute-start | bytes 786440 | tf_op jit(solution)/shard_map/while/body/eval_jaxpr/ppermute | solution.py:10
  515.6 10.0 %copy-start.3 = (bf16[2048,256]{1,0:T(8,128)(2,1)S(1)}, bf16[2048,256]{1,0:T(8,128)(2,1)}, u32[]{:S(2)}) copy-start(bf16[2048,256]{1,0:T(8,128)(2,1)} %copy-done.2) | copy-start | bytes 3145732 | tf_op jit(solution)/shard_map/while
  517.9 7.7 %collective-permute-start = (bf16[512,256]{0,1:T(8,128)(2,1)S(1)}, bf16[512,256]{0,1:T(8,128)(2,1)S(1)}, u32[]{:S(2)}, u32[]{:S(2)}) collective-permute-start(bf16[512,256]{0,1:T(8,128)(2,1)S(1)} %get-tuple-element.452), channel_id=1, source_target_pairs={{0,16},{16,32},{32,48},{48,64},{64,80},{80,96},{96,112},{1,17},{17... | collective-permute-start | bytes 786440 | tf_op jit(solution)/shard_map/while/body/eval_jaxpr/ppermute | solution.py:10
  (94 other events, 285.3 us)
Sparse Core Ops, SparseCore 0:
  10.1 200.1 all-gather.2
  527.5 64.4 all-reduce.1
where the time goes:
time: 605 us; the launch traced here: 600 us
  waiting for transfers between devices  304 us (50%)
  local copies, waits for them, and re-layouts  93.6 us (15%)
  starting transfers between devices  65.1 us (11%)
  other arithmetic  63.8 us (11%)
  matrix products  57.3 us (9%)
  between operations  14.2 us (2%)
    all_gather x1, waiting for transfers between devices, per_device(): everything = lax.all_gather(local_hist, 'group', axis=0, tiled=True)  202 us
    ppermute x15, starting transfers between devices, shifted(): return lax.ppermute(block, axis, route)  65 us
    psum x1, waiting for transfers between devices, spread(): return lax.psum(jnp.where(mine, array, jnp.zeros_like(array)), axis)  64.6 us
    ppermute x15, waiting for transfers between devices, shifted(): return lax.ppermute(block, axis, route)  36.3 us
    select_n x60, local copies, waits for them, and re-layouts, advance(): jnp.where(valid, lax.dynamic_update_index_in_dim(fresh, inputs, position,...  30.9 us
    dot_general x15, matrix products, sage_layer(): jnp.einsum('tij,tjh->tih', tiles, picked, preferred_element_type=jnp.floa...  30.1 us
    select_n x15, other arithmetic, advance(): jnp.where(valid, lax.dynamic_update_index_in_dim(finals, output, position...  28 us
    gather x1, local copies, waits for them, and re-layouts, per_device(): halo = jnp.take(everything, row_ids, axis=0)  21.9 us
  transfers between devices with their start and end apart: 17, of which 17 were waited for; matrix products, arithmetic and copies ran while one was open for 2% of the time, Pallas kernels for 0%

commit v1 on v0

v1 whole, which is shorter than its diff:
```python
import functools

import jax
import jax.numpy as jnp
from jax import lax
from jax.experimental import pallas as pl
from jax.experimental.pallas import tpu as pltpu
from jax.sharding import PartitionSpec as P

MESH = pl.DeviceIdType.MESH
F32 = jnp.float32
BF16 = jnp.bfloat16
SIDE = 4


def tile_table(targets, sources, blocks, span):
    count = targets.shape[1]
    key = targets * span + sources
    at = jnp.arange(count, dtype=jnp.int32)
    before = (key[:, None, :] < key[:, :, None]) | (
        (key[:, None, :] == key[:, :, None]) & (at[None, None, :] < at[None, :, None])
    )
    rank = jnp.sum(before.astype(jnp.int32), axis=2)
    placed = (rank[:, :, None] == at[None, None, :]).astype(jnp.int32)
    order = jnp.sum(placed * at[None, :, None], axis=1)
    halo = jnp.sum(placed * jnp.maximum(sources - blocks, 0)[:, :, None], axis=1)
    limits = (
        jnp.arange(blocks, dtype=jnp.int32)[:, None] * span
        + jnp.arange(blocks + 1, dtype=jnp.int32)[None, :]
    ).reshape(-1)
    limits = jnp.concatenate([limits, jnp.full((1,), blocks * span, jnp.int32)])
    starts = jnp.sum((key[:, :, None] < limits[None, None, :]).astype(jnp.int32), axis=1)
    return jnp.concatenate([order, halo, starts], axis=1)


def kernel(
    table,
    wanted,
    features,
    history,
    tiles,
    weight_self,
    weight_neigh,
    bias,
    gain,
    emb,
    fresh,
    idx,
    hist_v,
    tiles_v,
    halo_v,
    pack_v,
    dense_v,
    run_tile,
    run_prod,
    agg_v,
    cur_v,
    out_v,
    turn_v,
    ws_v,
    wn_v,
    local_sem,
    fresh_sem,
    own_sem,
    idx_send,
    idx_recv,
    halo_send,
    halo_recv,
    hop_send,
    hop_recv,
    emb_send,
    emb_recv,
):
    section = lax.axis_index("section")
    group = lax.axis_index("group")
    sections = lax.axis_size("section")
    groups = lax.axis_size("group")
    last = sections - 1
    micros = dense_v.shape[0]
    count = tiles_v.shape[0] // micros
    rows = dense_v.shape[1]
    half = rows // 2
    tile = tiles_v.shape[1]
    blocks = rows // tile
    share = emb.shape[0]
    gx, gy = group // SIDE, group % SIDE
    shifts = [(dx, dy) for dx in range(SIDE) for dy in range(SIDE) if dx or dy]

    def peer(shift):
        return ((gx + shift[0]) % SIDE) * SIDE + (gy + shift[1]) % SIDE

    def slot(shift):
        return shift[0] * SIDE + shift[1]

    def back(shift):
        return ((-shift[0]) % SIDE, (-shift[1]) % SIDE)

    hist_in = pltpu.make_async_copy(history, hist_v, local_sem.at[0])
    tiles_in = pltpu.make_async_copy(tiles, tiles_v, local_sem.at[1])
    ws_in = pltpu.make_async_copy(weight_self, ws_v, local_sem.at[2])
    wn_in = pltpu.make_async_copy(weight_neigh, wn_v, local_sem.at[3])
    feat_in = pltpu.make_async_copy(features, cur_v, local_sem.at[4])
    hist_in.start()
    ws_in.start()
    wn_in.start()

    @pl.when(section == 0)
    def _():
        feat_in.start()

    tiles_in.start()

    barrier = pltpu.get_barrier_semaphore()
    for shift in shifts:
        pl.semaphore_signal(barrier, inc=1, device_id={"group": peer(shift)}, device_id_type=MESH)

    @pl.when(section > 0)
    def _():
        pl.semaphore_signal(barrier, inc=1, device_id={"section": section - 1}, device_id_type=MESH)

    @pl.when(section < last)
    def _():
        pl.semaphore_signal(barrier, inc=1, device_id={"section": last}, device_id_type=MESH)
        pl.semaphore_wait(barrier, groups)

    @pl.when(section == last)
    def _():
        pl.semaphore_wait(barrier, groups - 1 + sections - 1)

    def idx_copy(shift, side):
        return pltpu.make_async_remote_copy(
            src_ref=wanted,
            dst_ref=idx.at[group if side == "send" else peer(shift)],
            send_sem=idx_send.at[slot(shift)],
            recv_sem=idx_recv.at[slot(shift if side == "send" else back(shift))],
            device_id={"group": peer(shift)},
            device_id_type=MESH,
        )

    def halo_copy(shift, side):
        return pltpu.make_async_remote_copy(
            src_ref=pack_v.at[slot(shift)],
            dst_ref=halo_v.at[group if side == "send" else peer(shift)],
            send_sem=halo_send.at[slot(shift)],
            recv_sem=halo_recv.at[slot(shift if side == "send" else back(shift))],
            device_id={"group": peer(shift)},
            device_id_type=MESH,
        )

    for shift in shifts:
        idx_copy(shift, "send").start()
    hist_in.wait()
    halo_v[group] = hist_v[wanted[0, group]]
    for shift in shifts:
        idx_copy(shift, "recv").wait_recv()
        pack_v[slot(shift)] = hist_v[idx[peer(shift), 0, group]]
        halo_copy(shift, "send").start()
    tiles_in.wait()

    zero_tile = jnp.zeros((tile, tile), F32)
    zero_prod = jnp.zeros((tile, ws_v.shape[0]), F32)
    run_tile[0] = zero_tile
    run_prod[0] = zero_prod

    def build(micro, carry):
        total = zero_tile
        for t in range(count):
            total = total + tiles_v[micro * count + table[micro, t]].astype(F32)
            run_tile[t + 1] = total
        for b in range(blocks):
            for s in range(blocks):
                at = 2 * count + b * (blocks + 1) + s
                cell = run_tile[table[micro, at + 1]] - run_tile[table[micro, at]]
                dense_v[micro, b * tile : (b + 1) * tile, s * tile : (s + 1) * tile] = cell.astype(BF16)
        return carry

    lax.fori_loop(0, micros, build, 0)

    for shift in shifts:
        halo_copy(shift, "recv").wait_recv()

    def far(micro):
        total = zero_prod
        for t in range(count):
            total = total + jnp.dot(
                tiles_v[micro * count + table[micro, t]],
                halo_v[table[micro, count + t]],
                preferred_element_type=F32,
            )
            run_prod[t + 1] = total
        for b in range(blocks):
            at = 2 * count + b * (blocks + 1) + blocks
            agg_v[b * tile : (b + 1) * tile] = run_prod[table[micro, at + 1]] - run_prod[table[micro, at]]

    def hop(micro, part):
        at = pl.ds(micro * rows + part * half, half)
        return pltpu.make_async_remote_copy(
            src_ref=out_v.at[at],
            dst_ref=cur_v.at[at],
            send_sem=hop_send.at[micro, part],
            recv_sem=hop_recv.at[micro, part],
            device_id={"section": jnp.minimum(section + 1, last)},
            device_id_type=MESH,
        )

    def emb_copy(micro, to):
        return pltpu.make_async_remote_copy(
            src_ref=turn_v.at[micro, pl.ds(to * share, share)],
            dst_ref=emb.at[:, pl.ds(micro * rows, rows)],
            send_sem=emb_send.at[micro, to],
            recv_sem=emb_recv.at[micro],
            device_id={"section": to},
            device_id_type=MESH,
        )

    def emb_own(micro):
        return pltpu.make_async_copy(
            turn_v.at[micro, pl.ds(last * share, share)],
            emb.at[:, pl.ds(micro * rows, rows)],
            own_sem.at[micro],
        )

    def keep(micro):
        at = pl.ds(micro * rows, rows)
        return pltpu.make_async_copy(cur_v.at[at], fresh.at[at], fresh_sem.at[micro])

    ws_in.wait()
    wn_in.wait()

    @pl.when(section == 0)
    def _():
        feat_in.wait()

    far(0)

    def advance(micro, carry):
        @pl.when(section > 0)
        def _():
            hop(micro, 0).wait_recv()
            hop(micro, 1).wait_recv()

        keep(micro).start()
        inputs = cur_v[pl.ds(micro * rows, rows)]
        for part in range(2):
            own = cur_v[pl.ds(micro * rows + part * half, half)]
            near = jnp.dot(dense_v[micro, part * half : (part + 1) * half], inputs, preferred_element_type=F32)
            aggregate = (agg_v[part * half : (part + 1) * half] + near).astype(BF16)
            pre = jnp.dot(own, ws_v[...], preferred_element_type=F32)
            pre = pre + jnp.dot(aggregate, wn_v[...], preferred_element_type=F32) + bias[...]
            center = pre - jnp.mean(pre, axis=1, keepdims=True)
            variance = jnp.mean(center * center, axis=1, keepdims=True)
            normed = center * lax.rsqrt(variance + 1e-05) * gain[...]
            result = own.astype(F32) + jnp.maximum(normed, 0.0)
            out_v[pl.ds(micro * rows + part * half, half)] = result.astype(BF16)

            @pl.when(section < last)
            def _():
                hop(micro, part).start()

            @pl.when(section == last)
            def _():
                turn_v[micro, :, part * half : (part + 1) * half] = result.T.astype(BF16)

        @pl.when(section == last)
        def _():
            for to in range(last):
                emb_copy(micro, to).start()
            emb_own(micro).start()

        @pl.when(micro < micros - 1)
        def _():
            far(micro + 1)

        return carry

    lax.fori_loop(0, micros, advance, 0)

    for shift in shifts:
        idx_copy(shift, "send").wait_send()
        halo_copy(shift, "send").wait_send()

    def finish(micro, carry):
        keep(micro).wait()

        @pl.when(section < last)
        def _():
            hop(micro, 0).wait_send()
            hop(micro, 1).wait_send()
            emb_copy(micro, 0).wait_recv()

        @pl.when(section == last)
        def _():
            for to in range(last):
                emb_copy(micro, to).wait_send()
            emb_own(micro).wait()

        return carry

    lax.fori_loop(0, micros, finish, 0)


def per_device(
    features, history, halo_blocks, tile_values, tile_dst, tile_src, w_self, w_neigh, bias, gain
):
    sections = lax.axis_size("section")
    groups = lax.axis_size("group")
    nodes, width = features.shape
    micros, count, tile = tile_values.shape[:3]
    rows = nodes // micros
    blocks = rows // tile
    share = width // sections
    table = tile_table(tile_dst, tile_src, blocks, blocks + groups)
    smem = pl.BlockSpec(memory_space=pltpu.SMEM)
    vmem = pl.BlockSpec(memory_space=pltpu.VMEM)
    hbm = pl.BlockSpec(memory_space=pl.ANY)
    emb, fresh = pl.pallas_call(
        kernel,
        out_shape=(
            jax.ShapeDtypeStruct((share, nodes), BF16),
            jax.ShapeDtypeStruct((nodes, width), BF16),
        ),
        in_specs=[smem, smem, hbm, hbm, hbm, hbm, hbm, vmem, vmem],
        out_specs=(hbm, hbm),
        scratch_shapes=[
            pltpu.SMEM((groups, 1, groups), jnp.int32),
            pltpu.VMEM((nodes // tile, tile, width), BF16),
            pltpu.VMEM((micros * count, tile, tile), BF16),
            pltpu.VMEM((groups, tile, width), BF16),
            pltpu.VMEM((groups, tile, width), BF16),
            pltpu.VMEM((micros, rows, rows), BF16),
            pltpu.VMEM((count + 1, tile, tile), F32),
            pltpu.VMEM((count + 1, tile, width), F32),
            pltpu.VMEM((rows, width), F32),
            pltpu.VMEM((nodes, width), BF16),
            pltpu.VMEM((nodes, width), BF16),
            pltpu.VMEM((micros, width, rows), BF16),
            pltpu.VMEM((width, width), BF16),
            pltpu.VMEM((width, width), BF16),
            pltpu.SemaphoreType.DMA((5,)),
            pltpu.SemaphoreType.DMA((micros,)),
            pltpu.SemaphoreType.DMA((micros,)),
            pltpu.SemaphoreType.DMA((groups,)),
            pltpu.SemaphoreType.DMA((groups,)),
            pltpu.SemaphoreType.DMA((groups,)),
            pltpu.SemaphoreType.DMA((groups,)),
            pltpu.SemaphoreType.DMA((micros, 2)),
            pltpu.SemaphoreType.DMA((micros, 2)),
            pltpu.SemaphoreType.DMA((micros, sections)),
            pltpu.SemaphoreType.DMA((micros,)),
        ],
        compiler_params=pltpu.CompilerParams(
            collective_id=0, has_side_effects=True, vmem_limit_bytes=52 * 1024 * 1024
        ),
    )(
        table,
        halo_blocks.reshape(1, groups),
        features,
        history.reshape(nodes // tile, tile, width),
        tile_values.reshape(micros * count, tile, tile),
        w_self[0],
        w_neigh[0],
        bias,
        gain,
    )
    return emb.T, fresh.reshape(1, nodes, width)


def solution(mesh):
    placed = (
        P("group", None),
        P("section", "group", None),
        P("group", None, None),
        P("group", None, None, None),
        P("group", None),
        P("group", None),
        P("section", None, None),
        P("section", None, None),
        P("section", None),
        P("section", None),
    )
    return jax.shard_map(
        per_device,
        mesh=mesh,
        in_specs=placed,
        out_specs=(P("group", "section"), P("section", "group", None)),
        check_vma=False,
    )
```

time: 605 us -> 87.7 us (0.14)
  waiting for transfers between devices: 304 us -> 0 us
  local copies, waits for them, and re-layouts: 93.6 us -> 7.74 us
  Pallas kernels: 0 us -> 77.2 us
  starting transfers between devices: 65.1 us -> 0 us
  other arithmetic: 63.8 us -> 1.91 us
  matrix products: 57.3 us -> 0 us
  between operations: 14.2 us -> 0.67 us
    all_gather x1 -> x0, waiting for transfers between devices: 202 us -> none  [per_device(): everything = lax.all_gather(local_hist, 'group', axis=0, tiled=True)]
    pallas_call x0 -> x1, Pallas kernels: none -> 77.2 us  [per_device(): pl.pallas_call(kernel, out_shape=(jax.ShapeDtypeStruct((share, nodes), BF...]
    ppermute x15 -> x0, starting transfers between devices: 65 us -> none  [shifted(): return lax.ppermute(block, axis, route)]
    psum x1 -> x0, waiting for transfers between devices: 64.6 us -> none  [spread(): return lax.psum(jnp.where(mine, array, jnp.zeros_like(array)), axis)]
    dot_general x60 -> x0, matrix products: 57.3 us -> none  [the longest x15 30.1 us: sage_layer(): jnp.einsum('tij,tjh->tih', tiles, picked, preferred_element_type=jnp.floa...]
    select_n x47 -> x0, other arithmetic: 50.2 us -> none  [the longest x15 28 us: advance(): jnp.where(valid, lax.dynamic_update_index_in_dim(finals, output, position...]
    ppermute x15 -> x0, waiting for transfers between devices: 36.3 us -> none  [shifted(): return lax.ppermute(block, axis, route)]
    select_n x76 -> x0, local copies, waits for them, and re-layouts: 34.5 us -> none  [the longest x60 30.9 us: advance(): jnp.where(valid, lax.dynamic_update_index_in_dim(fresh, inputs, position,...]
  transfers between devices with their start and end apart: 17 -> 0, of which waited for: 17 -> 0; matrix products, arithmetic and copies ran while one was open for 2% -> 0% of each run, Pallas kernels for 0% -> 0%
where the time goes in v1:
time: 87.7 us; the launch traced here: 87.5 us
  Pallas kernels  77.2 us (88%)
  local copies, waits for them, and re-layouts  7.74 us (9%)
  other arithmetic  1.91 us (2%)
    pallas_call x1, Pallas kernels, per_device(): pl.pallas_call(kernel, out_shape=(jax.ShapeDtypeStruct((share, nodes), BF...  77.2 us
    unnamed x12, local copies, waits for them, and re-layouts  7.58 us

profile of v1, /device:TPU:1, one launch (start us, length us, event | category | flops | bytes accessed | tf_op | source)
XLA Modules:
  0.0 87.5 jit_solution(2807879776641771575)
XLA Ops:
  0.6 0.1 iota_add_fusion
  0.7 0.1 add.25
  0.8 0.1 pad_add_fusion.1
  0.9 0.7 add_maximum_fusion
  1.6 0.3 convert_reduce_fusion
  1.9 0.2 select_reduce_fusion.1
  2.0 0.5 convert_reduce_fusion.1
  2.6 0.1 copy.12
  2.6 0.1 pad_add_fusion.table
  2.7 0.0 copy-start
  2.7 0.9 %copy-done = bf16[1,256,256]{2,1,0:T(8,128)(2,1)S(1)} copy-done((bf16[1,256,256]{2,1,0:T(8,128)(2,1)S(1)}, bf16[1,256,256]{2,1,0:T(8,128)(2,1)}, u32[]{:S(2)}) %copy-start) | copy-done | bytes 131096
  3.6 0.0 copy-start.1
  3.6 0.9 %copy-done.1 = bf16[1,256,256]{2,1,0:T(8,128)(2,1)S(1)} copy-done((bf16[1,256,256]{2,1,0:T(8,128)(2,1)S(1)}, bf16[1,256,256]{2,1,0:T(8,128)(2,1)}, u32[]{:S(2)}) %copy-start.1) | copy-done | bytes 131096
  4.5 0.0 copy-start.2
  4.5 0.7 copy-done.2
  5.2 0.0 copy-start.3
  5.2 0.7 copy-done.3
  5.9 0.0 copy-start.4
  5.9 0.7 copy-done.4
  6.6 77.2 %shard_map.113 = (bf16[32,4096]{1,0:T(8,128)(2,1)S(1)}, bf16[4096,256]{1,0:T(8,128)(2,1)}) custom-call(s32[8,85]{1,0:T(8,128)S(1)} %pad_add_fusion.table, s32[1,16]{1,0:T(1,128)S(1)} %bitcast.10, bf16[4096,256]{1,0:T(8,128)(2,1)} %features.1, bf16[32,128,256]{2,1,0:T(8,128)(2,1)} %bitcast.12, bf16[256,128,128]{2,1,0:T(8,128)(2,1)} %bitcast.11, ...), custom_call_target="tpu_custom_call" | custom-call | tf_op jit(solution)/shard_map/pallas_call | solution.py:316
  83.7 0.7 copy.15
  84.4 3.0 %copy.16 = bf16[1,4096,256]{2,1,0:T(8,128)(2,1)} copy(bf16[1,4096,256]{2,1,0:T(8,128)(2,1)} %bitcast.13) | data formatting | bytes 4194304
  (2 shorter events, 0.0 us)
Async XLA Ops:
  2.7 0.9 %copy-start = (bf16[1,256,256]{2,1,0:T(8,128)(2,1)S(1)}, bf16[1,256,256]{2,1,0:T(8,128)(2,1)}, u32[]{:S(2)}) copy-start(bf16[1,256,256]{2,1,0:T(8,128)(2,1)} %param.16) | copy-start | bytes 393220
  3.6 0.9 %copy-start.1 = (bf16[1,256,256]{2,1,0:T(8,128)(2,1)S(1)}, bf16[1,256,256]{2,1,0:T(8,128)(2,1)}, u32[]{:S(2)}) copy-start(bf16[1,256,256]{2,1,0:T(8,128)(2,1)} %param.17) | copy-start | bytes 393220
  4.5 0.7 copy-start.2
  5.2 0.7 copy-start.3
  5.9 0.7 copy-start.4

commit v2 on v1

v2 whole, which is shorter than its diff:
```python
import functools

import jax
import jax.numpy as jnp
from jax import lax
from jax.experimental import pallas as pl
from jax.experimental.pallas import tpu as pltpu
from jax.sharding import PartitionSpec as P

MESH = pl.DeviceIdType.MESH
F32 = jnp.float32
BF16 = jnp.bfloat16
SIDE = 4


def tile_table(targets, sources, blocks, span):
    micros, count = targets.shape
    key = targets * span + sources
    far_source = jnp.maximum(sources - blocks, 0)
    at = lax.broadcasted_iota(jnp.int32, (micros, count), 1)
    rank = jnp.zeros((micros, count), jnp.int32)
    for j in range(count):
        other = key[:, j : j + 1]
        rank = rank + jnp.where((other < key) | ((other == key) & (at > j)), 1, 0)
    lane = lax.broadcasted_iota(jnp.int32, (micros, 128), 1)
    place = jnp.where(lane < count, lane, lane - count)
    cell = lane - 2 * count
    block = sum(jnp.where(cell >= b * (blocks + 1), 1, 0) for b in range(1, blocks + 1))
    limit = block * span + cell - block * (blocks + 1)
    table = jnp.zeros((micros, 128), jnp.int32)
    for t in range(count):
        chosen = jnp.where(lane < count, t, far_source[:, t : t + 1])
        sorted_part = jnp.where(rank[:, t : t + 1] == place, chosen, 0)
        start_part = jnp.where(key[:, t : t + 1] < limit, 1, 0)
        table = table + jnp.where(lane < 2 * count, sorted_part, start_part)
    return table


def kernel(
    wanted,
    targets,
    sources,
    features,
    history,
    tiles,
    weight_self,
    weight_neigh,
    bias,
    gain,
    emb,
    fresh,
    idx,
    own_idx,
    table,
    table_v,
    dst_v,
    src_v,
    hist_v,
    tiles_v,
    halo_v,
    pack_v,
    dense_v,
    run_tile,
    run_prod,
    agg_v,
    stage_v,
    cur_v,
    mid_v,
    out_v,
    turn_v,
    ws_v,
    wn_v,
    bias_v,
    gain_v,
    local_sem,
    keep_sem,
    own_sem,
    idx_send,
    idx_recv,
    halo_send,
    halo_recv,
    hop_send,
    hop_recv,
    emb_send,
    emb_recv,
    pair_send,
    pair_recv,
    agg_send,
    agg_recv,
    give_send,
    give_recv,
):
    section = lax.axis_index("section")
    group = lax.axis_index("group")
    sections = lax.axis_size("section")
    groups = lax.axis_size("group")
    side = section % 2
    sibling = section + 1 - 2 * side
    first = section < 2
    top = section >= sections - 2
    micros = dense_v.shape[0]
    each = micros // 2
    count = tiles_v.shape[0] // micros
    rows = dense_v.shape[1]
    half = rows // 2
    tile = tiles_v.shape[1]
    blocks = rows // tile
    share = emb.shape[0]
    gx, gy = group // SIDE, group % SIDE
    shifts = [(dx, dy) for dx in range(SIDE) for dy in range(SIDE) if dx or dy]

    def peer(shift):
        return ((gx + shift[0]) % SIDE) * SIDE + (gy + shift[1]) % SIDE

    def slot(shift):
        return shift[0] * SIDE + shift[1]

    def back(shift):
        return ((-shift[0]) % SIDE, (-shift[1]) % SIDE)

    wanted_in = pltpu.make_async_copy(wanted, own_idx, local_sem.at[0])
    dst_in = pltpu.make_async_copy(targets, dst_v, local_sem.at[1])
    src_in = pltpu.make_async_copy(sources, src_v, local_sem.at[2])
    hist_in = pltpu.make_async_copy(history, hist_v, local_sem.at[3])
    feat_in = pltpu.make_async_copy(features, cur_v, local_sem.at[4])
    tiles_in = pltpu.make_async_copy(tiles, tiles_v, local_sem.at[5])
    params = [(weight_self, ws_v), (weight_neigh, wn_v), (bias, bias_v), (gain, gain_v)]
    params_in = [
        pltpu.make_async_copy(source, target.at[side], local_sem.at[6 + i])
        for i, (source, target) in enumerate(params)
    ]
    for copy in [wanted_in, dst_in, src_in, hist_in] + params_in:
        copy.start()

    @pl.when(section == 0)
    def _():
        feat_in.start()

    tiles_in.start()

    barrier = pltpu.get_barrier_semaphore()
    for shift in shifts:
        pl.semaphore_signal(barrier, inc=1, device_id={"group": peer(shift)}, device_id_type=MESH)
    for step in range(1, sections):
        pl.semaphore_signal(
            barrier, inc=1, device_id={"section": (section + step) % sections}, device_id_type=MESH
        )

    dst_in.wait()
    src_in.wait()
    table_v[...] = tile_table(dst_v[...], src_v[...], blocks, blocks + groups)
    table_in = pltpu.make_async_copy(table_v, table, local_sem.at[10])
    table_in.start()
    wanted_in.wait()
    pl.semaphore_wait(barrier, groups + sections - 2)

    def idx_copy(shift, way):
        return pltpu.make_async_remote_copy(
            src_ref=own_idx,
            dst_ref=idx.at[group if way == "send" else peer(shift)],
            send_sem=idx_send.at[slot(shift)],
            recv_sem=idx_recv.at[slot(shift if way == "send" else back(shift))],
            device_id={"group": peer(shift)},
            device_id_type=MESH,
        )

    def halo_copy(shift, way):
        return pltpu.make_async_remote_copy(
            src_ref=pack_v.at[slot(shift)],
            dst_ref=halo_v.at[group if way == "send" else peer(shift)],
            send_sem=halo_send.at[slot(shift)],
            recv_sem=halo_recv.at[slot(shift if way == "send" else back(shift))],
            device_id={"group": peer(shift)},
            device_id_type=MESH,
        )

    params_out = [
        pltpu.make_async_remote_copy(
            src_ref=source,
            dst_ref=target.at[side],
            send_sem=pair_send.at[i],
            recv_sem=pair_recv.at[i],
            device_id={"section": sibling},
            device_id_type=MESH,
        )
        for i, (source, target) in enumerate(params)
    ]

    for shift in shifts:
        idx_copy(shift, "send").start()
    hist_in.wait()
    halo_v[group] = hist_v[own_idx[0, group]]
    for shift in shifts:
        idx_copy(shift, "recv").wait_recv()
        pack_v[slot(shift)] = hist_v[idx[peer(shift), 0, group]]
        halo_copy(shift, "send").start()
    for copy in params_out:
        copy.start()
    tiles_in.wait()
    table_in.wait()

    zero_tile = jnp.zeros((tile, tile), F32)
    zero_prod = jnp.zeros((tile, ws_v.shape[1]), F32)
    run_tile[0] = zero_tile
    run_prod[0] = zero_prod

    def build(micro, carry):
        total = zero_tile
        for t in range(count):
            total = total + tiles_v[micro * count + table[micro, t]].astype(F32)
            run_tile[t + 1] = total
        for b in range(blocks):
            for s in range(blocks):
                at = 2 * count + b * (blocks + 1) + s
                cell = run_tile[table[micro, at + 1]] - run_tile[table[micro, at]]
                dense_v[micro, b * tile : (b + 1) * tile, s * tile : (s + 1) * tile] = cell.astype(BF16)
        return carry

    lax.fori_loop(0, micros, build, 0)

    for shift in shifts:
        halo_copy(shift, "recv").wait_recv()

    def far(micro, result):
        total = zero_prod
        for t in range(count):
            total = total + jnp.dot(
                tiles_v[micro * count + table[micro, t]],
                halo_v[table[micro, count + t]],
                preferred_element_type=F32,
            )
            run_prod[t + 1] = total
        for b in range(blocks):
            at = 2 * count + b * (blocks + 1) + blocks
            result[b * tile : (b + 1) * tile] = run_prod[table[micro, at + 1]] - run_prod[table[micro, at]]

    def layer(micro, source, near_from, result, step, part):
        at = pl.ds(micro * rows + part * half, half)
        own = source[at]
        near = jnp.dot(
            dense_v[micro, part * half : (part + 1) * half],
            source[pl.ds(micro * rows, rows)],
            preferred_element_type=F32,
        )
        aggregate = (near_from[part * half : (part + 1) * half] + near).astype(BF16)
        pre = jnp.dot(own, ws_v[step], preferred_element_type=F32)
        pre = pre + jnp.dot(aggregate, wn_v[step], preferred_element_type=F32) + bias_v[step]
        center = pre - jnp.mean(pre, axis=1, keepdims=True)
        variance = jnp.mean(center * center, axis=1, keepdims=True)
        normed = center * lax.rsqrt(variance + 1e-05) * gain_v[step]
        value = own.astype(F32) + jnp.maximum(normed, 0.0)
        if result is not None:
            result[at] = value.astype(BF16)
        return value

    def hop(micro, part):
        at = pl.ds(micro * rows + part * half, half)
        onward = jnp.where(section == 0, 1, jnp.where(section == 1, 2 + micro % 2, section + 2))
        return pltpu.make_async_remote_copy(
            src_ref=out_v.at[at],
            dst_ref=cur_v.at[at],
            send_sem=hop_send.at[micro, part],
            recv_sem=hop_recv.at[micro, part],
            device_id={"section": onward % sections},
            device_id_type=MESH,
        )

    def emb_copy(micro, step):
        to = (section + step) % sections
        return pltpu.make_async_remote_copy(
            src_ref=turn_v.at[micro, pl.ds(to * share, share)],
            dst_ref=emb.at[:, pl.ds(micro * rows, rows)],
            send_sem=emb_send.at[micro, step],
            recv_sem=emb_recv.at[micro],
            device_id={"section": to},
            device_id_type=MESH,
        )

    def emb_own(micro):
        return pltpu.make_async_copy(
            turn_v.at[micro, pl.ds(section * share, share)],
            emb.at[:, pl.ds(micro * rows, rows)],
            own_sem.at[micro],
        )

    def keep(micro, source):
        at = pl.ds(micro * rows, rows)
        return pltpu.make_async_copy(source.at[at], fresh.at[at], keep_sem.at[micro])

    def give(micro, source):
        at = pl.ds(micro * rows, rows)
        return pltpu.make_async_remote_copy(
            src_ref=source.at[at],
            dst_ref=fresh.at[at],
            send_sem=give_send.at[micro],
            recv_sem=give_recv.at[micro],
            device_id={"section": sibling},
            device_id_type=MESH,
        )

    def agg_copy(j):
        return pltpu.make_async_remote_copy(
            src_ref=stage_v.at[j],
            dst_ref=agg_v.at[side, j],
            send_sem=agg_send.at[j],
            recv_sem=agg_recv.at[j],
            device_id={"section": sibling},
            device_id_type=MESH,
        )

    for copy in params_in:
        copy.wait()

    @pl.when(first)
    def _():
        @pl.when(section == 0)
        def _():
            feat_in.wait()

        far(0, agg_v.at[0, 0])

        def advance(micro, carry):
            @pl.when(section > 0)
            def _():
                hop(micro, 0).wait_recv()
                hop(micro, 1).wait_recv()

            keep(micro, cur_v).start()
            for part in range(2):
                layer(micro, cur_v, agg_v.at[0, 0], out_v, side, part)
                hop(micro, part).start()

            @pl.when(micro < micros - 1)
            def _():
                far(micro + 1, agg_v.at[0, 0])

            return carry

        lax.fori_loop(0, micros, advance, 0)

    @pl.when(jnp.logical_not(first))
    def _():
        def prepare(j, carry):
            far(2 * j + 1 - side, stage_v.at[j])
            agg_copy(j).start()
            far(2 * j + side, agg_v.at[side, j])
            return carry

        lax.fori_loop(0, each, prepare, 0)
        for copy in params_out:
            copy.wait_recv()

        def advance(j, carry):
            micro = 2 * j + side
            agg_copy(j).wait_recv()
            hop(micro, 0).wait_recv()
            hop(micro, 1).wait_recv()
            for part in range(2):
                layer(micro, cur_v, agg_v.at[0, j], mid_v, 0, part)
            for part in range(2):
                value = layer(micro, mid_v, agg_v.at[1, j], out_v, 1, part)

                @pl.when(top)
                def _():
                    turn_v[micro, :, part * half : (part + 1) * half] = value.T.astype(BF16)

                @pl.when(jnp.logical_not(top))
                def _():
                    hop(micro, part).start()

            @pl.when(top)
            def _():
                for step in range(1, sections):
                    emb_copy(micro, step).start()
                emb_own(micro).start()

            @pl.when(side == 0)
            def _():
                keep(micro, cur_v).start()
                give(micro, mid_v).start()

            @pl.when(side == 1)
            def _():
                keep(micro, mid_v).start()
                give(micro, cur_v).start()

            return carry

        lax.fori_loop(0, each, advance, 0)

    for shift in shifts:
        idx_copy(shift, "send").wait_send()
        halo_copy(shift, "send").wait_send()
    for copy in params_out:
        copy.wait_send()

    @pl.when(first)
    def _():
        for copy in params_out:
            copy.wait_recv()

        def finish(micro, carry):
            keep(micro, cur_v).wait()
            hop(micro, 0).wait_send()
            hop(micro, 1).wait_send()
            return carry

        lax.fori_loop(0, micros, finish, 0)

    @pl.when(jnp.logical_not(first))
    def _():
        def finish(j, carry):
            micro = 2 * j + side
            agg_copy(j).wait_send()
            keep(micro, cur_v).wait()
            give(micro, cur_v).wait_send()
            give(2 * j + 1 - side, cur_v).wait_recv()

            @pl.when(jnp.logical_not(top))
            def _():
                hop(micro, 0).wait_send()
                hop(micro, 1).wait_send()

            @pl.when(top)
            def _():
                for step in range(1, sections):
                    emb_copy(micro, step).wait_send()
                emb_own(micro).wait()

            return carry

        lax.fori_loop(0, each, finish, 0)

    def collect(micro, carry):
        @pl.when(section != sections - 2 + micro % 2)
        def _():
            emb_copy(micro, 1).wait_recv()

        return carry

    lax.fori_loop(0, micros, collect, 0)


def per_device(
    features, history, halo_blocks, tile_values, tile_dst, tile_src, w_self, w_neigh, bias, gain
):
    sections = lax.axis_size("section")
    groups = lax.axis_size("group")
    nodes, width = features.shape
    micros, count, tile = tile_values.shape[:3]
    rows = nodes // micros
    share = width // sections
    dma = pltpu.SemaphoreType.DMA
    hbm = pl.BlockSpec(memory_space=pltpu.HBM)
    vmem = pl.BlockSpec(memory_space=pltpu.VMEM)
    emb, fresh = pl.pallas_call(
        kernel,
        out_shape=(
            pltpu.VMEM((share, nodes), BF16),
            pltpu.VMEM((nodes, width), BF16),
        ),
        in_specs=[hbm] * 10,
        out_specs=(vmem, vmem),
        scratch_shapes=[
            pltpu.SMEM((groups, 1, groups), jnp.int32),
            pltpu.SMEM((1, groups), jnp.int32),
            pltpu.SMEM((micros, 128), jnp.int32),
            pltpu.VMEM((micros, 128), jnp.int32),
            pltpu.VMEM((micros, count), jnp.int32),
            pltpu.VMEM((micros, count), jnp.int32),
            pltpu.VMEM((nodes // tile, tile, width), BF16),
            pltpu.VMEM((micros * count, tile, tile), BF16),
            pltpu.VMEM((groups, tile, width), BF16),
            pltpu.VMEM((groups, tile, width), BF16),
            pltpu.VMEM((micros, rows, rows), BF16),
            pltpu.VMEM((count + 1, tile, tile), F32),
            pltpu.VMEM((count + 1, tile, width), F32),
            pltpu.VMEM((2, micros // 2, rows, width), F32),
            pltpu.VMEM((micros // 2, rows, width), F32),
            pltpu.VMEM((nodes, width), BF16),
            pltpu.VMEM((nodes, width), BF16),
            pltpu.VMEM((nodes, width), BF16),
            pltpu.VMEM((micros, width, rows), BF16),
            pltpu.VMEM((2, width, width), BF16),
            pltpu.VMEM((2, width, width), BF16),
            pltpu.VMEM((2, 1, width), F32),
            pltpu.VMEM((2, 1, width), F32),
            dma((11,)),
            dma((micros,)),
            dma((micros,)),
            dma((groups,)),
            dma((groups,)),
            dma((groups,)),
            dma((groups,)),
            dma((micros, 2)),
            dma((micros, 2)),
            dma((micros, sections)),
            dma((micros,)),
            dma((4,)),
            dma((4,)),
            dma((micros // 2,)),
            dma((micros // 2,)),
            dma((micros,)),
            dma((micros,)),
        ],
        compiler_params=pltpu.CompilerParams(
            collective_id=0, has_side_effects=True, vmem_limit_bytes=60 * 1024 * 1024
        ),
    )(
        halo_blocks.reshape(1, groups),
        tile_dst,
        tile_src,
        features,
        history.reshape(nodes // tile, tile, width),
        tile_values.reshape(micros * count, tile, tile),
        w_self[0],
        w_neigh[0],
        bias,
        gain,
    )
    return emb.T, fresh.reshape(1, nodes, width)


def solution(mesh):
    placed = (
        P("group", None),
        P("section", "group", None),
        P("group", None, None),
        P("group", None, None, None),
        P("group", None),
        P("group", None),
        P("section", None, None),
        P("section", None, None),
        P("section", None),
        P("section", None),
    )
    return jax.shard_map(
        per_device,
        mesh=mesh,
        in_specs=placed,
        out_specs=(P("group", "section"), P("section", "group", None)),
        check_vma=False,
    )
```

time: 87.7 us -> 78.2 us (0.89)
  local copies, waits for them, and re-layouts: 7.74 us -> 2.02 us
  other arithmetic: 1.91 us -> 0 us
  Pallas kernels: 77.2 us -> 75.4 us
    unnamed x12 -> x2, local copies, waits for them, and re-layouts: 7.58 us -> 2.02 us
    pallas_call x1, Pallas kernels: 77.2 us -> 75.4 us  [per_device(): pl.pallas_call(kernel, out_shape=(pltpu.VMEM((share, nodes), BF16), pltpu...]
    reduce_sum x3 -> x0, other arithmetic: 0.96 us -> none  [the longest x1 0.51 us: tile_table(): jnp.sum((key[:, :, None] < limits[None, None, :]).astype(jnp.int32), axis=1)]
where the time goes in v2:
time: 78.2 us; the launch traced here: 78.1 us
  Pallas kernels  75.4 us (96%)
  local copies, waits for them, and re-layouts  2.02 us (3%)
    pallas_call x1, Pallas kernels, per_device(): pl.pallas_call(kernel, out_shape=(pltpu.VMEM((share, nodes), BF16), pltpu...  75.4 us
    unnamed x2, local copies, waits for them, and re-layouts  2.02 us

profile of v2, /device:TPU:1, one launch (start us, length us, event | category | flops | bytes accessed | tf_op | source)
XLA Modules:
  0.0 78.1 jit_solution(6686430649094290808)
XLA Ops:
  0.6 75.4 %shard_map.113 = (bf16[32,4096]{1,0:T(8,128)(2,1)S(1)}, bf16[4096,256]{1,0:T(8,128)(2,1)S(1)}) custom-call(s32[1,16]{1,0:T(1,128)} %bitcast.13, s32[8,32]{1,0:T(8,128)} %targets.1, s32[8,32]{1,0:T(8,128)} %sources.1, bf16[4096,256]{1,0:T(8,128)(2,1)} %features.1, bf16[32,128,256]{2,1,0:T(8,128)(2,1)} %bitcast.10, bf16[256,128,128]{2,1,0:T(8,128)(2,1)} %bitcast.9, ...), custom_call_target="tpu_custom_call" | custom-call | tf_op jit(solution)/shard_map/pallas_call | solution.py:456
  76.0 0.7 copy.14
  76.7 1.3 %copy.15 = bf16[1,4096,256]{2,1,0:T(8,128)(2,1)} copy(bf16[1,4096,256]{2,1,0:T(8,128)(2,1)S(1)} %bitcast.7) | data formatting | bytes 4194304

commit v3 on v2

--- a/solution.py
+++ b/solution.py
@@ -11,6 +11,7 @@
 F32 = jnp.float32
 BF16 = jnp.bfloat16
 SIDE = 4
+ALONE = ((6, 0), (7, 6))
 
 
 def tile_table(targets, sources, blocks, span):
@@ -89,17 +90,37 @@
     agg_recv,
     give_send,
     give_recv,
+    zx_v,
+    zagg_v,
+    zstage_v,
+    zws_v,
+    zwn_v,
+    zbias_v,
+    zgain_v,
+    zlocal,
+    zw_send,
+    zw_recv,
+    zagg_send,
+    zagg_recv,
+    zgive_send,
+    zgive_recv,
+    clear_sem,
 ):
     section = lax.axis_index("section")
     group = lax.axis_index("group")
     sections = lax.axis_size("section")
     groups = lax.axis_size("group")
+    last = sections - 1
     side = section % 2
     sibling = section + 1 - 2 * side
     first = section < 2
     top = section >= sections - 2
     micros = dense_v.shape[0]
-    each = micros // 2
+    relayed = micros - len(ALONE)
+    each = relayed // 2
+    owner = functools.reduce(jnp.logical_or, [section == device for _, device in ALONE])
+    mine = sum(jnp.where(section == device, z, 0) for z, (_, device) in enumerate(ALONE))
+    sole = sum(jnp.where(section == device, micro, 0) for micro, device in ALONE)
     count = tiles_v.shape[0] // micros
     rows = dense_v.shape[1]
     half = rows // 2
@@ -137,6 +158,16 @@
         feat_in.start()
 
     tiles_in.start()
+    zparams = [(weight_self, zws_v), (weight_neigh, zwn_v), (bias, zbias_v), (gain, zgain_v)]
+    zlocal_in = [
+        pltpu.make_async_copy(source, target.at[section], zlocal.at[i])
+        for i, (source, target) in enumerate(zparams)
+    ] + [pltpu.make_async_copy(features.at[pl.ds(sole * rows, rows)], zx_v.at[0], zlocal.at[4])]
+
+    @pl.when(owner)
+    def _():
+        for copy in zlocal_in:
+            copy.start()
 
     barrier = pltpu.get_barrier_semaphore()
     for shift in shifts:
@@ -185,6 +216,53 @@
         )
         for i, (source, target) in enumerate(params)
     ]
+
+    def zparam_copy(z, at, i):
+        source, target = zparams[i]
+        return pltpu.make_async_remote_copy(
+            src_ref=source,
+            dst_ref=target.at[at],
+            send_sem=zw_send.at[z, i],
+            recv_sem=zw_recv.at[at, i],
+            device_id={"section": ALONE[z][1]},
+            device_id_type=MESH,
+        )
+
+    def zagg_copy(z, at):
+        return pltpu.make_async_remote_copy(
+            src_ref=zstage_v.at[z],
+            dst_ref=zagg_v.at[at],
+            send_sem=zagg_send.at[z],
+            recv_sem=zagg_recv.at[at],
+            device_id={"section": ALONE[z][1]},
+            device_id_type=MESH,
+        )
+
+    def zgive(to):
+        return pltpu.make_async_remote_copy(
+            src_ref=zx_v.at[to],
+            dst_ref=fresh.at[pl.ds(sole * rows, rows)],
+            send_sem=zgive_send.at[to],
+            recv_sem=zgive_recv.at[mine],
+            device_id={"section": to},
+            device_id_type=MESH,
+        )
+
+    def zgot(z):
+        at = pl.ds(ALONE[z][0] * rows, rows)
+        return pltpu.make_async_remote_copy(
+            src_ref=fresh.at[at],
+            dst_ref=fresh.at[at],
+            send_sem=zgive_send.at[0],
+            recv_sem=zgive_recv.at[z],
+            device_id={"section": ALONE[z][1]},
+            device_id_type=MESH,
+        )
+
+    def zkeep(to):
+        return pltpu.make_async_copy(
+            zx_v.at[to], fresh.at[pl.ds(sole * rows, rows)], zlocal.at[5]
+        )
 
     for shift in shifts:
         idx_copy(shift, "send").start()
@@ -194,8 +272,19 @@
         idx_copy(shift, "recv").wait_recv()
         pack_v[slot(shift)] = hist_v[idx[peer(shift), 0, group]]
         halo_copy(shift, "send").start()
-    for copy in params_out:
-        copy.start()
+
+    @pl.when(jnp.logical_not(first))
+    def _():
+        for copy in params_out:
+            copy.start()
+
+    for z, (_, device) in enumerate(ALONE):
+
+        @pl.when(section != device)
+        def _():
+            for i in range(len(zparams)):
+                zparam_copy(z, section, i).start()
+
     tiles_in.wait()
     table_in.wait()
 
@@ -232,26 +321,92 @@
             run_prod[t + 1] = total
         for b in range(blocks):
             at = 2 * count + b * (blocks + 1) + blocks
-            result[b * tile : (b + 1) * tile] = run_prod[table[micro, at + 1]] - run_prod[table[micro, at]]
-
-    def layer(micro, source, near_from, result, step, part):
-        at = pl.ds(micro * rows + part * half, half)
-        own = source[at]
+            total = run_prod[table[micro, at + 1]] - run_prod[table[micro, at]]
+            result[b * tile : (b + 1) * tile] = total.astype(result.dtype)
+
+    def layer(micro, source, far_sum, ws, wn, offset, scale, part):
+        own = source[part * half : (part + 1) * half]
         near = jnp.dot(
-            dense_v[micro, part * half : (part + 1) * half],
-            source[pl.ds(micro * rows, rows)],
-            preferred_element_type=F32,
-        )
-        aggregate = (near_from[part * half : (part + 1) * half] + near).astype(BF16)
-        pre = jnp.dot(own, ws_v[step], preferred_element_type=F32)
-        pre = pre + jnp.dot(aggregate, wn_v[step], preferred_element_type=F32) + bias_v[step]
+            dense_v[micro, part * half : (part + 1) * half], source[...], preferred_element_type=F32
+        )
+        aggregate = (far_sum[part * half : (part + 1) * half].astype(F32) + near).astype(BF16)
+        pre = jnp.dot(own, ws[...], preferred_element_type=F32)
+        pre = pre + jnp.dot(aggregate, wn[...], preferred_element_type=F32) + offset[...]
         center = pre - jnp.mean(pre, axis=1, keepdims=True)
         variance = jnp.mean(center * center, axis=1, keepdims=True)
-        normed = center * lax.rsqrt(variance + 1e-05) * gain_v[step]
-        value = own.astype(F32) + jnp.maximum(normed, 0.0)
-        if result is not None:
-            result[at] = value.astype(BF16)
-        return value
+        normed = center * lax.rsqrt(variance + 1e-05) * scale[...]
+        return own.astype(F32) + jnp.maximum(normed, 0.0)
+
+    def paired(micro, source, far_sum, step, part):
+        return layer(
+            micro,
+            source.at[pl.ds(micro * rows, rows)],
+            far_sum,
+            ws_v.at[step],
+            wn_v.at[step],
+            bias_v.at[step],
+            gain_v.at[step],
+            part,
+        )
+
+    def zfar(z):
+        micro, device = ALONE[z]
+
+        @pl.when(section == device)
+        def _():
+            far(micro, zagg_v.at[section])
+
+        @pl.when(section != device)
+        def _():
+            far(micro, zstage_v.at[z])
+            zagg_copy(z, section).start()
+
+    def alone():
+        for copy in zlocal_in:
+            copy.wait()
+
+        def climb(depth, carry):
+            @pl.when(depth != section)
+            def _():
+                zagg_copy(0, depth).wait_recv()
+                for i in range(len(zparams)):
+                    zparam_copy(0, depth, i).wait_recv()
+
+            for part in range(2):
+                value = layer(
+                    sole,
+                    zx_v.at[depth],
+                    zagg_v.at[depth],
+                    zws_v.at[depth],
+                    zwn_v.at[depth],
+                    zbias_v.at[depth],
+                    zgain_v.at[depth],
+                    part,
+                )
+                zx_v[depth + 1, part * half : (part + 1) * half] = value.astype(BF16)
+
+            @pl.when(jnp.logical_and(depth < last, jnp.logical_and(section > 0, depth + 1 != section)))
+            def _():
+                zgive(depth + 1).start()
+
+            @pl.when(depth + 1 == section)
+            def _():
+                zkeep(depth + 1).start()
+
+            return carry
+
+        lax.fori_loop(0, sections, climb, 0)
+
+        @pl.when(section == 0)
+        def _():
+            pl.semaphore_wait(clear_sem, 1)
+            for to in range(1, sections):
+                zgive(to).start()
+
+        turn_v[sole] = zx_v[sections].astype(F32).T.astype(BF16)
+        for step in range(1, sections):
+            emb_copy(sole, step).start()
+        emb_own(sole).start()
 
     def hop(micro, part):
         at = pl.ds(micro * rows + part * half, half)
@@ -327,19 +482,48 @@
 
             keep(micro, cur_v).start()
             for part in range(2):
-                layer(micro, cur_v, agg_v.at[0, 0], out_v, side, part)
+                value = paired(micro, cur_v, agg_v.at[0, 0], side, part)
+                out_v[pl.ds(micro * rows + part * half, half)] = value.astype(BF16)
                 hop(micro, part).start()
 
-            @pl.when(micro < micros - 1)
+            @pl.when(micro < relayed - 1)
             def _():
                 far(micro + 1, agg_v.at[0, 0])
 
+            for z in range(len(ALONE)):
+
+                @pl.when(micro == z)
+                def _():
+                    zfar(z)
+
             return carry
 
-        lax.fori_loop(0, micros, advance, 0)
+        lax.fori_loop(0, relayed, advance, 0)
+
+        @pl.when(section == 0)
+        def _():
+            for micro, _ in ALONE:
+                keep(micro, cur_v).start()
+
+        @pl.when(section == 1)
+        def _():
+            def sent(micro, carry):
+                hop(micro, 0).wait_send()
+                hop(micro, 1).wait_send()
+                return carry
+
+            lax.fori_loop(0, relayed, sent, 0)
+            pl.semaphore_signal(clear_sem, inc=1, device_id={"section": sibling}, device_id_type=MESH)
+
+        @pl.when(owner)
+        def _():
+            alone()
 
     @pl.when(jnp.logical_not(first))
     def _():
+        for z in reversed(range(len(ALONE))):
+            zfar(z)
+
         def prepare(j, carry):
             far(2 * j + 1 - side, stage_v.at[j])
             agg_copy(j).start()
@@ -349,6 +533,10 @@
         lax.fori_loop(0, each, prepare, 0)
         for copy in params_out:
             copy.wait_recv()
+
+        @pl.when(owner)
+        def _():
+            alone()
 
         def advance(j, carry):
             micro = 2 * j + side
@@ -356,9 +544,10 @@
             hop(micro, 0).wait_recv()
             hop(micro, 1).wait_recv()
             for part in range(2):
-                layer(micro, cur_v, agg_v.at[0, j], mid_v, 0, part)
+                value = paired(micro, cur_v, agg_v.at[0, j], 0, part)
+                mid_v[pl.ds(micro * rows + part * half, half)] = value.astype(BF16)
             for part in range(2):
-                value = layer(micro, mid_v, agg_v.at[1, j], out_v, 1, part)
+                value = paired(micro, mid_v, agg_v.at[1, j], 1, part)
 
                 @pl.when(top)
                 def _():
@@ -366,6 +555,7 @@
 
                 @pl.when(jnp.logical_not(top))
                 def _():
+                    out_v[pl.ds(micro * rows + part * half, half)] = value.astype(BF16)
                     hop(micro, part).start()
 
             @pl.when(top)
@@ -391,24 +581,60 @@
     for shift in shifts:
         idx_copy(shift, "send").wait_send()
         halo_copy(shift, "send").wait_send()
-    for copy in params_out:
-        copy.wait_send()
-
     @pl.when(first)
     def _():
-        for copy in params_out:
-            copy.wait_recv()
-
         def finish(micro, carry):
             keep(micro, cur_v).wait()
-            hop(micro, 0).wait_send()
-            hop(micro, 1).wait_send()
+
+            @pl.when(section == 0)
+            def _():
+                hop(micro, 0).wait_send()
+                hop(micro, 1).wait_send()
+
             return carry
 
-        lax.fori_loop(0, micros, finish, 0)
+        lax.fori_loop(0, relayed, finish, 0)
+
+        @pl.when(section == 0)
+        def _():
+            for micro, _ in ALONE:
+                keep(micro, cur_v).wait()
+
+    for z, (_, device) in enumerate(ALONE):
+
+        @pl.when(section != device)
+        def _():
+            for i in range(len(zparams)):
+                zparam_copy(z, section, i).wait_send()
+            zagg_copy(z, section).wait_send()
+
+            @pl.when(section > 0)
+            def _():
+                zgot(z).wait_recv()
+
+    @pl.when(owner)
+    def _():
+        def given(to, carry):
+            @pl.when(to != section)
+            def _():
+                zgive(to).wait_send()
+
+            @pl.when(to == section)
+            def _():
+                zkeep(to).wait()
+
+            return carry
+
+        lax.fori_loop(1, sections, given, 0)
+        for step in range(1, sections):
+            emb_copy(sole, step).wait_send()
+        emb_own(sole).wait()
 
     @pl.when(jnp.logical_not(first))
     def _():
+        for copy in params_out:
+            copy.wait_send()
+
         def finish(j, carry):
             micro = 2 * j + side
             agg_copy(j).wait_send()
@@ -438,7 +664,12 @@
 
         return carry
 
-    lax.fori_loop(0, micros, collect, 0)
+    lax.fori_loop(0, relayed, collect, 0)
+    for micro, device in ALONE:
+
+        @pl.when(section != device)
+        def _():
+            emb_copy(micro, 1).wait_recv()
 
 
 def per_device(
@@ -502,6 +733,21 @@
             dma((micros // 2,)),
             dma((micros,)),
             dma((micros,)),
+            pltpu.VMEM((sections + 1, rows, width), BF16),
+            pltpu.VMEM((sections, rows, width), BF16),
+            pltpu.VMEM((len(ALONE), rows, width), BF16),
+            pltpu.VMEM((sections, width, width), BF16),
+            pltpu.VMEM((sections, width, width), BF16),
+            pltpu.VMEM((sections, 1, width), F32),
+            pltpu.VMEM((sections, 1, width), F32),
+            dma((6,)),
+            dma((len(ALONE), 4)),
+            dma((sections, 4)),
+            dma((len(ALONE),)),
+            dma((sections,)),
+            dma((sections,)),
+            dma((len(ALONE),)),
+            pltpu.SemaphoreType.REGULAR,
         ],
         compiler_params=pltpu.CompilerParams(
             collective_id=0, has_side_effects=True, vmem_limit_bytes=60 * 1024 * 1024

time: 78.2 us -> 73.2 us (0.936)
  Pallas kernels: 75.4 us -> 70.4 us
    pallas_call x1, Pallas kernels: 75.4 us -> 70.4 us  [per_device(): pl.pallas_call(kernel, out_shape=(pltpu.VMEM((share, nodes), BF16), pltpu...]
where the time goes in v3:
time: 73.2 us; the launch traced here: 73.1 us
  Pallas kernels  70.4 us (96%)
  local copies, waits for them, and re-layouts  2.02 us (3%)
    pallas_call x1, Pallas kernels, per_device(): pl.pallas_call(kernel, out_shape=(pltpu.VMEM((share, nodes), BF16), pltpu...  70.4 us
    unnamed x2, local copies, waits for them, and re-layouts  2.02 us

profile of v3, /device:TPU:1, one launch (start us, length us, event | category | flops | bytes accessed | tf_op | source)
XLA Modules:
  0.0 73.1 jit_solution(7412459678847087114)
XLA Ops:
  0.6 70.4 %shard_map.113 = (bf16[32,4096]{1,0:T(8,128)(2,1)S(1)}, bf16[4096,256]{1,0:T(8,128)(2,1)S(1)}) custom-call(s32[1,16]{1,0:T(1,128)} %bitcast.13, s32[8,32]{1,0:T(8,128)} %targets.1, s32[8,32]{1,0:T(8,128)} %sources.1, bf16[4096,256]{1,0:T(8,128)(2,1)} %features.1, bf16[32,128,256]{2,1,0:T(8,128)(2,1)} %bitcast.10, bf16[256,128,128]{2,1,0:T(8,128)(2,1)} %bitcast.9, ...), custom_call_target="tpu_custom_call" | custom-call | tf_op jit(solution)/shard_map/pallas_call | solution.py:687
  71.1 0.7 copy.14
  71.8 1.3 %copy.15 = bf16[1,4096,256]{2,1,0:T(8,128)(2,1)} copy(bf16[1,4096,256]{2,1,0:T(8,128)(2,1)S(1)} %bitcast.7) | data formatting | bytes 4194304

commit v4 on v3

--- a/solution.py
+++ b/solution.py
@@ -11,7 +11,8 @@
 F32 = jnp.float32
 BF16 = jnp.bfloat16
 SIDE = 4
-ALONE = ((6, 0), (7, 6))
+ORDER = (4, 5, 3, 6, 2, 7, 1)
+ALONE = ((6, 6), (7, 0))
 
 
 def tile_table(targets, sources, blocks, span):
@@ -104,6 +105,7 @@
     zagg_recv,
     zgive_send,
     zgive_recv,
+    zpass_send,
     clear_sem,
 ):
     section = lax.axis_index("section")
@@ -117,13 +119,17 @@
     top = section >= sections - 2
     micros = dense_v.shape[0]
     relayed = micros - len(ALONE)
-    each = relayed // 2
+    each = (relayed + 1) // 2
+    devices = [device for _, device in ALONE]
+    twins = [device for device in devices if device ^ 1 in devices]
+    twin = functools.reduce(jnp.logical_or, [section == device for device in twins], section < 0)
     owner = functools.reduce(jnp.logical_or, [section == device for _, device in ALONE])
     mine = sum(jnp.where(section == device, z, 0) for z, (_, device) in enumerate(ALONE))
     sole = sum(jnp.where(section == device, micro, 0) for micro, device in ALONE)
     count = tiles_v.shape[0] // micros
     rows = dense_v.shape[1]
     half = rows // 2
+    slab = half // 2
     tile = tiles_v.shape[1]
     blocks = rows // tile
     share = emb.shape[0]
@@ -158,11 +164,10 @@
         feat_in.start()
 
     tiles_in.start()
-    zparams = [(weight_self, zws_v), (weight_neigh, zwn_v), (bias, zbias_v), (gain, zgain_v)]
+    zparams = [(ws_v, zws_v), (wn_v, zwn_v), (bias_v, zbias_v), (gain_v, zgain_v)]
     zlocal_in = [
-        pltpu.make_async_copy(source, target.at[section], zlocal.at[i])
-        for i, (source, target) in enumerate(zparams)
-    ] + [pltpu.make_async_copy(features.at[pl.ds(sole * rows, rows)], zx_v.at[0], zlocal.at[4])]
+        pltpu.make_async_copy(features.at[pl.ds(sole * rows, rows)], zx_v.at[0], zlocal.at[4])
+    ]
 
     @pl.when(owner)
     def _():
@@ -176,6 +181,17 @@
         pl.semaphore_signal(
             barrier, inc=1, device_id={"section": (section + step) % sections}, device_id_type=MESH
         )
+
+    for copy in params_in:
+        copy.wait()
+    for target in (ws_v, wn_v, bias_v):
+        raw = target[side].astype(F32)
+        target[side] = (raw - jnp.mean(raw, axis=1, keepdims=True)).astype(target.dtype)
+
+    @pl.when(owner)
+    def _():
+        for source, target in zparams:
+            target[section] = source[side]
 
     dst_in.wait()
     src_in.wait()
@@ -207,7 +223,7 @@
 
     params_out = [
         pltpu.make_async_remote_copy(
-            src_ref=source,
+            src_ref=target.at[side],
             dst_ref=target.at[side],
             send_sem=pair_send.at[i],
             recv_sem=pair_recv.at[i],
@@ -220,12 +236,30 @@
     def zparam_copy(z, at, i):
         source, target = zparams[i]
         return pltpu.make_async_remote_copy(
-            src_ref=source,
+            src_ref=source.at[side],
             dst_ref=target.at[at],
             send_sem=zw_send.at[z, i],
             recv_sem=zw_recv.at[at, i],
             device_id={"section": ALONE[z][1]},
             device_id_type=MESH,
+        )
+
+    def zparam_pass(at, i):
+        target = zparams[i][1]
+        return pltpu.make_async_remote_copy(
+            src_ref=target.at[at],
+            dst_ref=target.at[at],
+            send_sem=zpass_send.at[at, i],
+            recv_sem=zw_recv.at[at, i],
+            device_id={"section": sibling},
+            device_id_type=MESH,
+        )
+
+    def direct(device):
+        if device not in twins:
+            return section != device
+        return jnp.logical_and(
+            section != device, jnp.logical_or(side == device % 2, section == device ^ 1)
         )
 
     def zagg_copy(z, at):
@@ -280,7 +314,7 @@
 
     for z, (_, device) in enumerate(ALONE):
 
-        @pl.when(section != device)
+        @pl.when(direct(device))
         def _():
             for i in range(len(zparams)):
                 zparam_copy(z, section, i).start()
@@ -324,20 +358,19 @@
             total = run_prod[table[micro, at + 1]] - run_prod[table[micro, at]]
             result[b * tile : (b + 1) * tile] = total.astype(result.dtype)
 
-    def layer(micro, source, far_sum, ws, wn, offset, scale, part):
-        own = source[part * half : (part + 1) * half]
+    def layer(micro, source, far_sum, ws, wn, offset, scale, at):
+        own = source[at * slab : (at + 1) * slab]
         near = jnp.dot(
-            dense_v[micro, part * half : (part + 1) * half], source[...], preferred_element_type=F32
-        )
-        aggregate = (far_sum[part * half : (part + 1) * half].astype(F32) + near).astype(BF16)
+            dense_v[micro, at * slab : (at + 1) * slab], source[...], preferred_element_type=F32
+        )
+        aggregate = (far_sum[at * slab : (at + 1) * slab].astype(F32) + near).astype(BF16)
         pre = jnp.dot(own, ws[...], preferred_element_type=F32)
         pre = pre + jnp.dot(aggregate, wn[...], preferred_element_type=F32) + offset[...]
-        center = pre - jnp.mean(pre, axis=1, keepdims=True)
-        variance = jnp.mean(center * center, axis=1, keepdims=True)
-        normed = center * lax.rsqrt(variance + 1e-05) * scale[...]
+        variance = jnp.mean(pre * pre, axis=1, keepdims=True)
+        normed = pre * lax.rsqrt(variance + 1e-05) * scale[...]
         return own.astype(F32) + jnp.maximum(normed, 0.0)
 
-    def paired(micro, source, far_sum, step, part):
+    def paired(micro, source, far_sum, step, at):
         return layer(
             micro,
             source.at[pl.ds(micro * rows, rows)],
@@ -346,7 +379,7 @@
             wn_v.at[step],
             bias_v.at[step],
             gain_v.at[step],
-            part,
+            at,
         )
 
     def zfar(z):
@@ -365,14 +398,36 @@
         for copy in zlocal_in:
             copy.wait()
 
+        @pl.when(twin)
+        def _():
+            def onward(at, carry):
+                depth = 2 * at + side
+
+                @pl.when(depth != section)
+                def _():
+                    for i in range(len(zparams)):
+                        zparam_copy(0, depth, i).wait_recv()
+                        zparam_pass(depth, i).start()
+
+                return carry
+
+            lax.fori_loop(0, sections // 2, onward, 0)
+
         def climb(depth, carry):
             @pl.when(depth != section)
             def _():
                 zagg_copy(0, depth).wait_recv()
+
+            @pl.when(
+                jnp.logical_and(
+                    depth != section, jnp.logical_or(jnp.logical_not(twin), depth % 2 != side)
+                )
+            )
+            def _():
                 for i in range(len(zparams)):
                     zparam_copy(0, depth, i).wait_recv()
 
-            for part in range(2):
+            for at in range(4):
                 value = layer(
                     sole,
                     zx_v.at[depth],
@@ -381,9 +436,9 @@
                     zwn_v.at[depth],
                     zbias_v.at[depth],
                     zgain_v.at[depth],
-                    part,
+                    at,
                 )
-                zx_v[depth + 1, part * half : (part + 1) * half] = value.astype(BF16)
+                zx_v[depth + 1, at * slab : (at + 1) * slab] = value.astype(BF16)
 
             @pl.when(jnp.logical_and(depth < last, jnp.logical_and(section > 0, depth + 1 != section)))
             def _():
@@ -403,8 +458,8 @@
             for to in range(1, sections):
                 zgive(to).start()
 
-        turn_v[sole] = zx_v[sections].astype(F32).T.astype(BF16)
-        for step in range(1, sections):
+        turn_v[sole] = turned(zx_v[sections])
+        for step in ORDER:
             emb_copy(sole, step).start()
         emb_own(sole).start()
 
@@ -431,6 +486,16 @@
             device_id_type=MESH,
         )
 
+    def turned(block):
+        width = block.shape[1]
+        row = lax.broadcasted_iota(jnp.int32, (width, width), 0)
+        column = lax.broadcasted_iota(jnp.int32, (width, width), 1)
+        unit = jnp.where(row == column, 1.0, 0.0).astype(BF16)
+        product = lax.dot_general(
+            unit, block, (((1,), (1,)), ((), ())), preferred_element_type=F32
+        )
+        return product.astype(BF16)
+
     def emb_own(micro):
         return pltpu.make_async_copy(
             turn_v.at[micro, pl.ds(section * share, share)],
@@ -463,9 +528,6 @@
             device_id_type=MESH,
         )
 
-    for copy in params_in:
-        copy.wait()
-
     @pl.when(first)
     def _():
         @pl.when(section == 0)
@@ -482,8 +544,9 @@
 
             keep(micro, cur_v).start()
             for part in range(2):
-                value = paired(micro, cur_v, agg_v.at[0, 0], side, part)
-                out_v[pl.ds(micro * rows + part * half, half)] = value.astype(BF16)
+                for at in range(part * 2, (part + 1) * 2):
+                    value = paired(micro, cur_v, agg_v.at[0, 0], side, at)
+                    out_v[pl.ds(micro * rows + at * slab, slab)] = value.astype(BF16)
                 hop(micro, part).start()
 
             @pl.when(micro < relayed - 1)
@@ -521,13 +584,19 @@
 
     @pl.when(jnp.logical_not(first))
     def _():
-        for z in reversed(range(len(ALONE))):
+        for z in range(len(ALONE)):
             zfar(z)
 
         def prepare(j, carry):
-            far(2 * j + 1 - side, stage_v.at[j])
-            agg_copy(j).start()
-            far(2 * j + side, agg_v.at[side, j])
+            @pl.when(2 * j + 1 - side < relayed)
+            def _():
+                far(2 * j + 1 - side, stage_v.at[j])
+                agg_copy(j).start()
+
+            @pl.when(2 * j + side < relayed)
+            def _():
+                far(2 * j + side, agg_v.at[side, j])
+
             return carry
 
         lax.fori_loop(0, each, prepare, 0)
@@ -538,29 +607,31 @@
         def _():
             alone()
 
-        def advance(j, carry):
+        def one_pair(j):
             micro = 2 * j + side
             agg_copy(j).wait_recv()
             hop(micro, 0).wait_recv()
             hop(micro, 1).wait_recv()
+            for at in range(4):
+                value = paired(micro, cur_v, agg_v.at[0, j], 0, at)
+                mid_v[pl.ds(micro * rows + at * slab, slab)] = value.astype(BF16)
             for part in range(2):
-                value = paired(micro, cur_v, agg_v.at[0, j], 0, part)
-                mid_v[pl.ds(micro * rows + part * half, half)] = value.astype(BF16)
-            for part in range(2):
-                value = paired(micro, mid_v, agg_v.at[1, j], 1, part)
+                for at in range(part * 2, (part + 1) * 2):
+                    value = paired(micro, mid_v, agg_v.at[1, j], 1, at)
+                    out_v[pl.ds(micro * rows + at * slab, slab)] = value.astype(BF16)
 
                 @pl.when(top)
                 def _():
-                    turn_v[micro, :, part * half : (part + 1) * half] = value.T.astype(BF16)
+                    at = pl.ds(micro * rows + part * half, half)
+                    turn_v[micro, :, part * half : (part + 1) * half] = turned(out_v[at])
 
                 @pl.when(jnp.logical_not(top))
                 def _():
-                    out_v[pl.ds(micro * rows + part * half, half)] = value.astype(BF16)
                     hop(micro, part).start()
 
             @pl.when(top)
             def _():
-                for step in range(1, sections):
+                for step in ORDER:
                     emb_copy(micro, step).start()
                 emb_own(micro).start()
 
@@ -573,6 +644,11 @@
             def _():
                 keep(micro, mid_v).start()
                 give(micro, cur_v).start()
+
+        def advance(j, carry):
+            @pl.when(2 * j + side < relayed)
+            def _():
+                one_pair(j)
 
             return carry
 
@@ -602,10 +678,13 @@
 
     for z, (_, device) in enumerate(ALONE):
 
-        @pl.when(section != device)
+        @pl.when(direct(device))
         def _():
             for i in range(len(zparams)):
                 zparam_copy(z, section, i).wait_send()
+
+        @pl.when(section != device)
+        def _():
             zagg_copy(z, section).wait_send()
 
             @pl.when(section > 0)
@@ -626,6 +705,21 @@
             return carry
 
         lax.fori_loop(1, sections, given, 0)
+
+        @pl.when(twin)
+        def _():
+            def passed(at, carry):
+                depth = 2 * at + side
+
+                @pl.when(depth != section)
+                def _():
+                    for i in range(len(zparams)):
+                        zparam_pass(depth, i).wait_send()
+
+                return carry
+
+            lax.fori_loop(0, sections // 2, passed, 0)
+
         for step in range(1, sections):
             emb_copy(sole, step).wait_send()
         emb_own(sole).wait()
@@ -637,21 +731,27 @@
 
         def finish(j, carry):
             micro = 2 * j + side
-            agg_copy(j).wait_send()
-            keep(micro, cur_v).wait()
-            give(micro, cur_v).wait_send()
-            give(2 * j + 1 - side, cur_v).wait_recv()
-
-            @pl.when(jnp.logical_not(top))
-            def _():
-                hop(micro, 0).wait_send()
-                hop(micro, 1).wait_send()
-
-            @pl.when(top)
-            def _():
-                for step in range(1, sections):
-                    emb_copy(micro, step).wait_send()
-                emb_own(micro).wait()
+
+            @pl.when(2 * j + 1 - side < relayed)
+            def _():
+                agg_copy(j).wait_send()
+                give(2 * j + 1 - side, cur_v).wait_recv()
+
+            @pl.when(micro < relayed)
+            def _():
+                keep(micro, cur_v).wait()
+                give(micro, cur_v).wait_send()
+
+                @pl.when(jnp.logical_not(top))
+                def _():
+                    hop(micro, 0).wait_send()
+                    hop(micro, 1).wait_send()
+
+                @pl.when(top)
+                def _():
+                    for step in range(1, sections):
+                        emb_copy(micro, step).wait_send()
+                    emb_own(micro).wait()
 
             return carry
 
@@ -747,6 +847,7 @@
             dma((sections,)),
             dma((sections,)),
             dma((len(ALONE),)),
+            dma((sections, 4)),
             pltpu.SemaphoreType.REGULAR,
         ],
         compiler_params=pltpu.CompilerParams(

time: 73.2 us -> 72 us (0.984)
  Pallas kernels: 70.4 us -> 69.2 us
    pallas_call x1, Pallas kernels: 70.4 us -> 69.2 us  [per_device(): pl.pallas_call(kernel, out_shape=(pltpu.VMEM((share, nodes), BF16), pltpu...]
where the time goes in v4:
time: 72 us; the launch traced here: 71.9 us
  Pallas kernels  69.2 us (96%)
  local copies, waits for them, and re-layouts  2.02 us (3%)
    pallas_call x1, Pallas kernels, per_device(): pl.pallas_call(kernel, out_shape=(pltpu.VMEM((share, nodes), BF16), pltpu...  69.2 us
    unnamed x2, local copies, waits for them, and re-layouts  2.02 us

profile of v4, /device:TPU:1, one launch (start us, length us, event | category | flops | bytes accessed | tf_op | source)
XLA Modules:
  0.0 71.9 jit_solution(16821354498027263632)
XLA Ops:
  0.6 69.2 %shard_map.113 = (bf16[32,4096]{1,0:T(8,128)(2,1)S(1)}, bf16[4096,256]{1,0:T(8,128)(2,1)S(1)}) custom-call(s32[1,16]{1,0:T(1,128)} %bitcast.13, s32[8,32]{1,0:T(8,128)} %targets.1, s32[8,32]{1,0:T(8,128)} %sources.1, bf16[4096,256]{1,0:T(8,128)(2,1)} %features.1, bf16[32,128,256]{2,1,0:T(8,128)(2,1)} %bitcast.10, bf16[256,128,128]{2,1,0:T(8,128)(2,1)} %bitcast.9, ...), custom_call_target="tpu_custom_call" | custom-call | tf_op jit(solution)/shard_map/pallas_call | solution.py:787
  69.9 0.7 copy.14
  70.6 1.3 %copy.15 = bf16[1,4096,256]{2,1,0:T(8,128)(2,1)} copy(bf16[1,4096,256]{2,1,0:T(8,128)(2,1)S(1)} %bitcast.7) | data formatting | bytes 4194304

commit v5 on v4

--- a/solution.py
+++ b/solution.py
@@ -463,14 +463,14 @@
             emb_copy(sole, step).start()
         emb_own(sole).start()
 
-    def hop(micro, part):
-        at = pl.ds(micro * rows + part * half, half)
+    def hop(micro):
+        at = pl.ds(micro * rows, rows)
         onward = jnp.where(section == 0, 1, jnp.where(section == 1, 2 + micro % 2, section + 2))
         return pltpu.make_async_remote_copy(
             src_ref=out_v.at[at],
             dst_ref=cur_v.at[at],
-            send_sem=hop_send.at[micro, part],
-            recv_sem=hop_recv.at[micro, part],
+            send_sem=hop_send.at[micro],
+            recv_sem=hop_recv.at[micro],
             device_id={"section": onward % sections},
             device_id_type=MESH,
         )
@@ -539,15 +539,13 @@
         def advance(micro, carry):
             @pl.when(section > 0)
             def _():
-                hop(micro, 0).wait_recv()
-                hop(micro, 1).wait_recv()
+                hop(micro).wait_recv()
 
             keep(micro, cur_v).start()
-            for part in range(2):
-                for at in range(part * 2, (part + 1) * 2):
-                    value = paired(micro, cur_v, agg_v.at[0, 0], side, at)
-                    out_v[pl.ds(micro * rows + at * slab, slab)] = value.astype(BF16)
-                hop(micro, part).start()
+            for at in range(4):
+                value = paired(micro, cur_v, agg_v.at[0, 0], side, at)
+                out_v[pl.ds(micro * rows + at * slab, slab)] = value.astype(BF16)
+            hop(micro).start()
 
             @pl.when(micro < relayed - 1)
             def _():
@@ -571,8 +569,7 @@
         @pl.when(section == 1)
         def _():
             def sent(micro, carry):
-                hop(micro, 0).wait_send()
-                hop(micro, 1).wait_send()
+                hop(micro).wait_send()
                 return carry
 
             lax.fori_loop(0, relayed, sent, 0)
@@ -610,27 +607,21 @@
         def one_pair(j):
             micro = 2 * j + side
             agg_copy(j).wait_recv()
-            hop(micro, 0).wait_recv()
-            hop(micro, 1).wait_recv()
+            hop(micro).wait_recv()
             for at in range(4):
                 value = paired(micro, cur_v, agg_v.at[0, j], 0, at)
                 mid_v[pl.ds(micro * rows + at * slab, slab)] = value.astype(BF16)
-            for part in range(2):
-                for at in range(part * 2, (part + 1) * 2):
-                    value = paired(micro, mid_v, agg_v.at[1, j], 1, at)
-                    out_v[pl.ds(micro * rows + at * slab, slab)] = value.astype(BF16)
-
-                @pl.when(top)
-                def _():
-                    at = pl.ds(micro * rows + part * half, half)
-                    turn_v[micro, :, part * half : (part + 1) * half] = turned(out_v[at])
-
-                @pl.when(jnp.logical_not(top))
-                def _():
-                    hop(micro, part).start()
+            for at in range(4):
+                value = paired(micro, mid_v, agg_v.at[1, j], 1, at)
+                out_v[pl.ds(micro * rows + at * slab, slab)] = value.astype(BF16)
+
+            @pl.when(jnp.logical_not(top))
+            def _():
+                hop(micro).start()
 
             @pl.when(top)
             def _():
+                turn_v[micro] = turned(out_v[pl.ds(micro * rows, rows)])
                 for step in ORDER:
                     emb_copy(micro, step).start()
                 emb_own(micro).start()
@@ -664,8 +655,7 @@
 
             @pl.when(section == 0)
             def _():
-                hop(micro, 0).wait_send()
-                hop(micro, 1).wait_send()
+                hop(micro).wait_send()
 
             return carry
 
@@ -744,8 +734,7 @@
 
                 @pl.when(jnp.logical_not(top))
                 def _():
-                    hop(micro, 0).wait_send()
-                    hop(micro, 1).wait_send()
+                    hop(micro).wait_send()
 
                 @pl.when(top)
                 def _():
@@ -823,8 +812,8 @@
             dma((groups,)),
             dma((groups,)),
             dma((groups,)),
-            dma((micros, 2)),
-            dma((micros, 2)),
+            dma((micros,)),
+            dma((micros,)),
             dma((micros, sections)),
             dma((micros,)),
             dma((4,)),

time: 72 us -> 71.5 us (level)
  no operation moved by 1% of the time
where the time goes in v5:
time: 71.5 us; the launch traced here: 71.4 us
  Pallas kernels  68.7 us (96%)
  local copies, waits for them, and re-layouts  2.02 us (3%)
    pallas_call x1, Pallas kernels, per_device(): pl.pallas_call(kernel, out_shape=(pltpu.VMEM((share, nodes), BF16), pltpu...  68.7 us
    unnamed x2, local copies, waits for them, and re-layouts  2.02 us

profile of v5, /device:TPU:1, one launch (start us, length us, event | category | flops | bytes accessed | tf_op | source)
XLA Modules:
  0.0 71.4 jit_solution(11025300880498691486)
XLA Ops:
  0.6 68.7 %shard_map.113 = (bf16[32,4096]{1,0:T(8,128)(2,1)S(1)}, bf16[4096,256]{1,0:T(8,128)(2,1)S(1)}) custom-call(s32[1,16]{1,0:T(1,128)} %bitcast.13, s32[8,32]{1,0:T(8,128)} %targets.1, s32[8,32]{1,0:T(8,128)} %sources.1, bf16[4096,256]{1,0:T(8,128)(2,1)} %features.1, bf16[32,128,256]{2,1,0:T(8,128)(2,1)} %bitcast.10, bf16[256,128,128]{2,1,0:T(8,128)(2,1)} %bitcast.9, ...), custom_call_target="tpu_custom_call" | custom-call | tf_op jit(solution)/shard_map/pallas_call | solution.py:776
  69.3 0.7 copy.14
  70.0 1.3 %copy.15 = bf16[1,4096,256]{2,1,0:T(8,128)(2,1)} copy(bf16[1,4096,256]{2,1,0:T(8,128)(2,1)S(1)} %bitcast.7) | data formatting | bytes 4194304

commit v6 on v5

--- a/solution.py
+++ b/solution.py
@@ -307,18 +307,6 @@
         pack_v[slot(shift)] = hist_v[idx[peer(shift), 0, group]]
         halo_copy(shift, "send").start()
 
-    @pl.when(jnp.logical_not(first))
-    def _():
-        for copy in params_out:
-            copy.start()
-
-    for z, (_, device) in enumerate(ALONE):
-
-        @pl.when(direct(device))
-        def _():
-            for i in range(len(zparams)):
-                zparam_copy(z, section, i).start()
-
     tiles_in.wait()
     table_in.wait()
 
@@ -340,6 +328,18 @@
         return carry
 
     lax.fori_loop(0, micros, build, 0)
+
+    @pl.when(jnp.logical_not(first))
+    def _():
+        for copy in params_out:
+            copy.start()
+
+    for z, (_, device) in enumerate(ALONE):
+
+        @pl.when(direct(device))
+        def _():
+            for i in range(len(zparams)):
+                zparam_copy(z, section, i).start()
 
     for shift in shifts:
         halo_copy(shift, "recv").wait_recv()

time: 71.5 us -> 72 us (level)
  no operation moved by 1% of the time
where the time goes in v6:
time: 72 us; the launch traced here: 71.9 us
  Pallas kernels  69.2 us (96%)
  local copies, waits for them, and re-layouts  2.02 us (3%)
    pallas_call x1, Pallas kernels, per_device(): pl.pallas_call(kernel, out_shape=(pltpu.VMEM((share, nodes), BF16), pltpu...  69.2 us
    unnamed x2, local copies, waits for them, and re-layouts  2.02 us

profile of v6, /device:TPU:1, one launch (start us, length us, event | category | flops | bytes accessed | tf_op | source)
XLA Modules:
  0.0 71.9 jit_solution(3686115995848045130)
XLA Ops:
  0.6 69.2 %shard_map.113 = (bf16[32,4096]{1,0:T(8,128)(2,1)S(1)}, bf16[4096,256]{1,0:T(8,128)(2,1)S(1)}) custom-call(s32[1,16]{1,0:T(1,128)} %bitcast.13, s32[8,32]{1,0:T(8,128)} %targets.1, s32[8,32]{1,0:T(8,128)} %sources.1, bf16[4096,256]{1,0:T(8,128)(2,1)} %features.1, bf16[32,128,256]{2,1,0:T(8,128)(2,1)} %bitcast.10, bf16[256,128,128]{2,1,0:T(8,128)(2,1)} %bitcast.9, ...), custom_call_target="tpu_custom_call" | custom-call | tf_op jit(solution)/shard_map/pallas_call | solution.py:776
  69.8 0.7 copy.14
  70.5 1.3 %copy.15 = bf16[1,4096,256]{2,1,0:T(8,128)(2,1)} copy(bf16[1,4096,256]{2,1,0:T(8,128)(2,1)S(1)} %bitcast.7) | data formatting | bytes 4194304
